TPU v7x, 512 devices: a whole 4x4x16 slice. The times are simulated.
512 devices in a mesh: row: 32 (over z, core), col: 16 (over x, y).
Axes of the slice: x: 4, y: 4, z: 16, core: 2. Of those that a mesh axis runs over, the one named last changes fastest.
Arguments:
- panel_t: float32 [256, 131072], P('col', 'row'), may hold values from -1 to 1
- trailing: float32 [131072, 2048], P('row', 'col'), may hold values from -6 to 6
Outputs:
- r_factor: float32 [256, 256], replicated
- top_rows: float32 [256, 2048], P(None, 'col')
- updated: float32 [131072, 2048], P('row', 'col')
All inputs are finite; a program needn't handle non-finite values.
Results may differ from a plain program's by a relative error of at most 0.00011.
Values sent between devices are 32-bit elements; how exact they have to be, the bound alone decides.
A program may use at most 128 MiB of HBM per device.

v0:
```python
import jax
import jax.numpy as jnp
from jax import lax
from jax.sharding import PartitionSpec as P

HIGHEST = lax.Precision.HIGHEST


def merged(value, axis, join):
    pieces = lax.all_gather(value, axis)
    head = pieces[0]
    tail = pieces[1:]
    subtotal, _ = lax.scan(lambda subtotal, slab: (join(subtotal, slab), None), head, tail)
    return subtotal


def gram_of(factor_rows):
    return lax.dot_general(
        factor_rows,
        factor_rows,
        (((1,), (1,)), ((), ())),
        precision=HIGHEST,
        preferred_element_type=jnp.float32,
    )


def stacked_factor(first_factor, second_factor):
    joined = lax.dot_general(
        first_factor,
        first_factor,
        (((0,), (0,)), ((), ())),
        precision=HIGHEST,
        preferred_element_type=jnp.float32,
    )
    joined = joined + lax.dot_general(
        second_factor,
        second_factor,
        (((0,), (0,)), ((), ())),
        precision=HIGHEST,
        preferred_element_type=jnp.float32,
    )
    return jnp.linalg.cholesky(joined).T


def body(panel_t, trailing):
    gathered = lax.all_gather(panel_t, "col", axis=0, tiled=True)
    gram_local = gram_of(gathered)
    projection = jnp.dot(gathered, trailing, precision=HIGHEST, preferred_element_type=jnp.float32)
    leaf_factor = jnp.linalg.cholesky(gram_local).T
    upper_factor = merged(leaf_factor, "row", stacked_factor)
    projection = lax.psum(projection, "row")
    lower_factor = upper_factor.T
    top_rows = lax.linalg.triangular_solve(lower_factor, projection, left_side=True, lower=True)
    coeffs = lax.linalg.triangular_solve(
        lower_factor, top_rows, left_side=True, lower=True, transpose_a=True
    )
    change = lax.dot_general(
        gathered,
        coeffs,
        (((0,), (0,)), ((), ())),
        precision=HIGHEST,
        preferred_element_type=jnp.float32,
    )
    return (upper_factor, top_rows, trailing - change)


def solution(mesh):
    placed = (P("col", "row"), P("row", "col"))
    return jax.shard_map(
        body,
        mesh=mesh,
        in_specs=placed,
        out_specs=(P(), P(None, "col"), P("row", "col")),
        check_vma=False,
    )
```

profile of v0, /device:TPU:1, one launch (start us, length us, event | category | flops | bytes accessed | tf_op | source)
XLA Modules:
  0.0 1448.8 jit_solution(5344106646364415715)
XLA Ops:
  8.0 75.2 %all-gather.4.cloned.1.call-done = f32[256,4096]{1,0:T(8,128)} async-done(((f32[16,4096]{1,0:T(8,128)}), f32[256,4096]{1,0:T(8,128)}) %all-gather.4.cloned.1.call-update) | async-done | bytes 4194320 | tf_op jit(solution)/shard_map/all_gather | solution.py:46
  83.2 12.2 fusion.25
  95.6 11.7 cholesky.164
  117.7 11.7 cholesky.181
  140.1 71.9 %all-gather.6.cloned.1.call-done = f32[8192,256]{0,1:T(8,128)} async-done(((f32[256,256]{0,1:T(8,128)}), f32[8192,256]{0,1:T(8,128)}) %all-gather.6.cloned.1.call-update) | async-done | bytes 8388624 | tf_op jit(solution)/shard_map/all_gather | solution.py:10
  227.9 1177.0 %while.11 = (s32[]{:T(128)}, f32[256,256]{0,1:T(8,128)S(1)}, f32[31,256,256]{2,1,0:T(8,128)}, s32[]{:T(128)}, f32[]{:T(128)}) while((s32[]{:T(128)}, f32[256,256]{0,1:T(8,128)S(1)}, f32[31,256,256]{2,1,0:T(8,128)}, s32[]{:T(128)}, f32[]{:T(128)}) %tuple.69), condition=%wide.region_5.7_spmd, body=%wide.region_4.6_spmd.sunk | while | flops 453525760 | bytes 4393043 | solution.py:13
  230.2 11.7 cholesky.347
  252.2 11.7 cholesky.349
  268.1 11.7 cholesky.347
  290.2 11.7 cholesky.349
  306.1 11.7 cholesky.347
  328.2 11.7 cholesky.349
  344.1 11.7 cholesky.347
  366.2 11.7 cholesky.349
  382.1 11.7 cholesky.347
  404.1 11.7 cholesky.349
  420.0 11.7 cholesky.347
  442.1 11.7 cholesky.349
  458.0 11.7 cholesky.347
  480.1 11.7 cholesky.349
  495.9 11.7 cholesky.347
  518.0 11.7 cholesky.349
  533.9 11.7 cholesky.347
  556.0 11.7 cholesky.349
  571.9 11.7 cholesky.347
  594.0 11.7 cholesky.349
  609.9 11.7 cholesky.347
  631.9 11.7 cholesky.349
  647.8 11.7 cholesky.347
  669.9 11.7 cholesky.349
  685.8 11.7 cholesky.347
  707.9 11.7 cholesky.349
  723.8 11.7 cholesky.347
  745.8 11.7 cholesky.349
  761.7 11.7 cholesky.347
  783.8 11.7 cholesky.349
  799.7 11.7 cholesky.347
  821.8 11.7 cholesky.349
  837.7 11.7 cholesky.347
  859.7 11.7 cholesky.349
  875.6 11.7 cholesky.347
  897.7 11.7 cholesky.349
  913.6 11.7 cholesky.347
  935.6 11.7 cholesky.349
  951.6 11.7 cholesky.347
  973.7 11.7 cholesky.349
  989.6 11.7 cholesky.347
  1011.6 11.7 cholesky.349
  1027.5 11.7 cholesky.347
  1049.6 11.7 cholesky.349
  1065.5 11.7 cholesky.347
  1087.6 11.7 cholesky.349
  1103.4 11.7 cholesky.347
  1125.5 11.7 cholesky.349
  1141.4 11.7 cholesky.347
  1163.5 11.7 cholesky.349
  1179.4 11.7 cholesky.347
  1201.5 11.7 cholesky.349
  1239.5 11.7 cholesky.349
  1277.4 11.7 cholesky.349
  1315.4 11.7 cholesky.349
  1353.3 11.7 cholesky.349
  1391.3 11.7 cholesky.349
  1410.0 19.7 %custom-call.13 = f32[2,128,128]{1,2,0:T(8,128)S(1)} custom-call(f32[2,128,128]{2,1,0:T(8,128)S(1)} %get-tuple-element.29), custom_call_target="InvertDiagBlocksLowerTriangular" | custom-call | tf_op jit(solution)/shard_map/triangular_solve | solution.py:53
  (457 shorter events, 527.7 us)
Async XLA Ops:
  7.2 76.0 %all-gather.4.cloned.1.call-start = ((), (), s32[]{:S(2)}) async-start(), calls=%async_computation | async-start | bytes 4456448 | tf_op jit(solution)/shard_map/all_gather | solution.py:46
  7.9 124.3 %copy-start = (f32[4096,128]{1,0:T(8,128)S(1)}, f32[4096,128]{1,0:T(8,128)}, u32[]{:S(2)}) copy-start(f32[4096,128]{1,0:T(8,128)} %param.6) | copy-start | bytes 6291460
  7.9 204.1 %all-gather.6.cloned.1.call-start = ((), (), s32[]{:S(2)}) async-start(), calls=%async_computation.2 | async-start | bytes 8650752 | tf_op jit(solution)/shard_map/all_gather | solution.py:10
  132.1 1297.6 %all-reduce.3.cloned.1.call-start = ((), (), s32[]{:S(2)}) async-start(), calls=%async_computation.1 | async-start | bytes 262144 | tf_op jit(solution)/shard_map/psum | solution.py:51
  219.0 8.9 slice-start
  1404.9 28.6 %copy-start.1 = (f32[4096,128]{0,1:T(8,128)S(1)}, f32[4096,128]{0,1:T(8,128)}, u32[]{:S(2)}) copy-start(f32[4096,128]{0,1:T(8,128)} %copy.18) | copy-start | bytes 6291460
Sparse Core Ops, SparseCore 0:
  11.0 72.1 all-gather.3
  132.2 79.7 all-gather.5
  215.0 193.3 all-reduce.2
where the time goes:
time: 1450 us
  other arithmetic  1110 us (77%)
  waiting for transfers between devices  148 us (10%)
  matrix products  106 us (7%)
  loops' own time  39.9 us (3%)
  local copies, waits for them, and re-layouts  30.7 us (2%)
  between operations  15.2 us (1%)
    another operation x186, other arithmetic, stacked_factor(): return jnp.linalg.cholesky(joined).T  1050 us
    all_gather x1, waiting for transfers between devices, body(): gathered = lax.all_gather(panel_t, 'col', axis=0, tiled=True)  75.2 us
    all_gather x1, waiting for transfers between devices, merged(): pieces = lax.all_gather(value, axis)  71.9 us
    dot_general x31, matrix products, stacked_factor(): lax.dot_general(second_factor, second_factor, (((0,), (0,)), ((), ())), p...  50.7 us
    another operation x1, loops' own time, merged(): lax.scan(lambda subtotal, slab: (join(subtotal, slab), None), head, tail)  39.9 us
    another operation x6, other arithmetic, body(): leaf_factor = jnp.linalg.cholesky(gram_local).T  33.9 us
  transfers between devices with their start and end apart: 3, of which 2 were waited for; matrix products, arithmetic and copies ran while one was open for 82% of the time, Pallas kernels for 0%

commit v1 on v0

v1 whole, which is shorter than its diff:
```python
import jax
import jax.numpy as jnp
from jax import lax
from jax.experimental import pallas as pl
from jax.experimental.pallas import tpu as pltpu
from jax.sharding import PartitionSpec as P

MESH = pl.DeviceIdType.MESH
K = 4096
H = K // 2
S1P, S1M, F1P, F1M = 0, 1, 2, 3
S2P, S2M, F2P, F2M = 4, 9, 14, 18
NMSG = 22

class Half:
    def __init__(self, half, panel, g, ssem, rsem, x, y):
        self.h, self.panel, self.g, self.ss, self.rs = half, panel, g, ssem, rsem
        self.p, self.q = (x, y) if half == 0 else (y, x)
        w = lambda v: lax.rem(v, 4)
        self.P = [self.p, w(self.p + 3), w(self.p + 1), w(self.p + 2)]
        self.Q = [self.q, w(self.q + 3), w(self.q + 1), w(self.q + 2)]
        self.pending = []
    def col(self, p, q):
        return p * 4 + q if self.h == 0 else q * 4 + p
    def slc(self, p, q, lo, n):
        r = pl.multiple_of(self.col(p, q) * 16 + 8 * self.h, 8)
        return self.g.at[pl.ds(r, 8), pl.ds(lo, n)]
    def send(self, m, p, q, lo, n, axis, sign, own=False):
        dst = self.slc(p, q, lo, n)
        src = self.panel.at[pl.ds(8 * self.h, 8), pl.ds(lo, n)] if own else dst
        i = 1 if sign < 0 else 2
        to = self.col(self.P[i], self.q) if axis == 1 else self.col(self.p, self.Q[i])
        c = pltpu.make_async_remote_copy(src, dst, self.ss.at[self.h, m], self.rs.at[self.h, m], device_id={"col": to}, device_id_type=MESH)
        c.start()
        self.pending.append(c)
    def recv(self, m, p, q, lo, n):
        d = self.slc(p, q, lo, n)
        pltpu.make_async_remote_copy(d, d, self.ss.at[self.h, m], self.rs.at[self.h, m], device_id={"col": self.col(self.P[1], self.q)}, device_id_type=MESH).wait_recv()
    def start_own(self):
        self.send(S1P, self.p, self.q, 0, K, 1, 1, True)
        self.send(S1M, self.p, self.q, 0, K, 1, -1, True)
    def start_own2(self):
        self.send(S2P, self.p, self.q, 0, K, 2, 1, True)
        self.send(S2M, self.p, self.q, 0, K, 2, -1, True)
    def first_p(self):
        pm = self.P[1]
        self.recv(S1P, pm, self.q, 0, K)
        self.send(F1P, pm, self.q, 0, H, 1, 1)
        self.send(S2P + 1, pm, self.q, 0, K, 2, 1)
        self.send(S2M + 1, pm, self.q, 0, K, 2, -1)
    def first_m(self):
        pp = self.P[2]
        self.recv(S1M, pp, self.q, 0, K)
        self.send(F1M, pp, self.q, H, H, 1, -1)
        self.send(S2P + 2, pp, self.q, 0, K, 2, 1)
        self.send(S2M + 2, pp, self.q, 0, K, 2, -1)
    def far(self):
        po = self.P[3]
        self.recv(F1P, po, self.q, 0, H)
        self.send(S2P + 3, po, self.q, 0, H, 2, 1)
        self.send(S2M + 3, po, self.q, 0, H, 2, -1)
        self.recv(F1M, po, self.q, H, H)
        self.send(S2P + 4, po, self.q, H, H, 2, 1)
        self.send(S2M + 4, po, self.q, H, H, 2, -1)
    def second(self, s):
        ps = self.P[s]
        if s < 3:
            self.recv(S2P + s, ps, self.Q[1], 0, K)
            self.send(F2P + s, ps, self.Q[1], 0, H, 2, 1)
            self.recv(S2M + s, ps, self.Q[2], 0, K)
            self.send(F2M + s, ps, self.Q[2], H, H, 2, -1)
        else:
            self.recv(S2P + 3, ps, self.Q[1], 0, H)
            self.send(F2P + 3, ps, self.Q[1], 0, H, 2, 1)
            self.recv(S2M + 3, ps, self.Q[2], 0, H)
            self.recv(S2P + 4, ps, self.Q[1], H, H)
            self.recv(S2M + 4, ps, self.Q[2], H, H)
            self.send(F2M + 3, ps, self.Q[2], H, H, 2, -1)
    def last(self, s):
        ps, qo = self.P[s], self.Q[3]
        self.recv(F2P + s, ps, qo, 0, H)
        self.recv(F2M + s, ps, qo, H, H)


HI = lax.Precision.HIGHEST
NC = 16

def dot(a, b, ca=1, cb=0):
    return lax.dot_general(a, b, (((ca,), (cb,)), ((), ())), precision=HI, preferred_element_type=jnp.float32)

def rcopy(src, dst, ss, rs, **dev):
    return pltpu.make_async_remote_copy(src, dst, ss, rs, device_id=dev, device_id_type=MESH)

def make_kernel(NR):
    NZ = NR // 2
    PW = 32 // NR
    PZ = 128 // NZ
    def kernel(panel, trail, g, psum, gram, ssem, rsem, lsem, xb, gp, rs16, gs, rs32, ga, gall, pp, pex, prs, pown, qs, qr):
        c = lax.axis_index("col")
        w = lax.axis_index("row")
        x, y = c // 4, lax.rem(c, 4)
        z, core = w // 2, lax.rem(w, 2)
        sib = z * 2 + 1 - core
        own = pltpu.make_async_copy(panel, g.at[pl.ds(pl.multiple_of(c * 16, 16), 16), :], lsem.at[0])
        own.start()
        mine = pltpu.make_async_copy(panel.at[:, pl.ds(pl.multiple_of(c * 256, 256), 256)], xb.at[pl.ds(pl.multiple_of(c * 16, 16), 16), :], lsem.at[1])
        mine.start()
        A = Half(0, panel, g, ssem, rsem, x, y)
        B = Half(1, panel, g, ssem, rsem, x, y)
        bar = pltpu.get_barrier_semaphore()
        for i in range(1, NC):
            pl.semaphore_signal(bar, inc=1, device_id={"col": lax.rem(c + i, NC)}, device_id_type=MESH)
        for i in range(1, NR):
            pl.semaphore_signal(bar, inc=1, device_id={"row": lax.rem(w + i, NR)}, device_id_type=MESH)
        pl.semaphore_wait(bar, NC + NR - 2)
        for i in range(1, NC):
            j = lax.rem(c + i, NC)
            rcopy(panel.at[:, pl.ds(pl.multiple_of(j * 256, 256), 256)], xb.at[pl.ds(pl.multiple_of(c * 16, 16), 16), :], qs.at[0], qr.at[0], col=j).start()
        A.start_own(); B.start_own(); A.start_own2(); B.start_own2()
        def wait_bytes(ref, k, send):
            d = rcopy(ref, ref, qs.at[k], qr.at[k], col=lax.rem(c + 1, NC))
            d.wait_send() if send else d.wait_recv()
        mine.wait()
        wait_bytes(xb.at[pl.ds(0, 240), :], 0, False)
        xv = xb[...]
        gp[...] = dot(xv, xv, 1, 1)
        for i in range(1, NC):
            j = lax.rem(c + i, NC)
            rcopy(gp.at[pl.ds(pl.multiple_of(j * 16, 16), 16), :], rs16.at[i - 1], qs.at[1], qr.at[1], col=j).start()
        A.first_p(); B.first_p(); A.first_m(); B.first_m()
        wait_bytes(rs16, 1, False)
        acc = gp[pl.ds(pl.multiple_of(c * 16, 16), 16), :]
        for i in range(NC - 1):
            acc = acc + rs16[i]
        for h in range(2):
            for r in range(16):
                gs[h * 16 + r] = acc[r:r + 1, 128 * h:128 * h + 128]
        for i in range(1, NR):
            j = lax.rem(w + i, NR)
            rcopy(gs.at[pl.ds(j * PW, PW)], rs32.at[pl.ds((i - 1) * PW, PW)], qs.at[2], qr.at[2], row=j).start()
        A.second(0); B.second(0)
        wait_bytes(rs32, 2, False)
        tot = gs[pl.ds(w * PW, PW)]
        for i in range(NR - 1):
            tot = tot + rs32[pl.ds(i * PW, PW)]
        ga[pl.ds(w * PW, PW)] = tot
        for i in range(1, NR):
            j = lax.rem(w + i, NR)
            rcopy(ga.at[pl.ds(w * PW, PW)], ga.at[pl.ds(w * PW, PW)], qs.at[3], qr.at[3], row=j).start()
        A.far(); B.far()
        wait_bytes(ga.at[pl.ds(0, 32 - PW)], 3, False)
        for i in range(1, NC):
            j = lax.rem(c + i, NC)
            rcopy(ga, gall.at[c], qs.at[4], qr.at[4], col=j).start()
        gall[c] = ga[...]
        for s in (1, 2, 3):
            A.second(s); B.second(s)
        wait_bytes(gall.at[pl.ds(0, 15)], 4, False)
        for b in range(NC):
            for h in range(2):
                for t in range(2):
                    gram[16 * b + 8 * t:16 * b + 8 * t + 8, 128 * h:128 * h + 128] = gall[b, 16 * h + 8 * t:16 * h + 8 * t + 8, 0, :]
        for s in range(4):
            A.last(s); B.last(s)
        own.wait()
        pp[...] = jnp.zeros_like(pp)
        CH = 512
        @pl.loop(0, K // CH)
        def _(i):
            k0 = pl.multiple_of(i * CH, CH)
            pp[...] += dot(g[:, pl.ds(k0, CH)], trail[pl.ds(k0, CH), :])
        ex = rcopy(pp.at[pl.ds(pl.multiple_of((1 - core) * 128, 128), 128), :], pex, qs.at[5], qr.at[5], row=sib)
        ex.start(); ex.wait_recv()
        pex[...] += pp[pl.ds(pl.multiple_of(core * 128, 128), 128), :]
        for i in range(1, NZ):
            j = lax.rem(z + i, NZ)
            rcopy(pex.at[pl.ds(pl.multiple_of(j * PZ, PZ), PZ), :], prs.at[pl.ds((i - 1) * PZ, PZ), :], qs.at[6], qr.at[6], row=j * 2 + core).start()
        wait_bytes(prs, 6, False)
        tot = pex[pl.ds(pl.multiple_of(z * PZ, PZ), PZ), :]
        for i in range(NZ - 1):
            tot = tot + prs[i * PZ:(i + 1) * PZ, :]
        me = pl.multiple_of(core * 128 + z * PZ, PZ)
        psum[pl.ds(me, PZ), :] = tot
        for i in range(1, NZ):
            j = lax.rem(z + i, NZ)
            rcopy(psum.at[pl.ds(me, PZ), :], psum.at[pl.ds(me, PZ), :], qs.at[7], qr.at[7], row=j * 2 + core).start()
        wait_bytes(psum.at[pl.ds(0, 128 - PZ), :], 7, False)
        half = psum.at[pl.ds(pl.multiple_of(core * 128, 128), 128), :]
        back = rcopy(half, half, qs.at[8], qr.at[8], row=sib)
        back.start(); back.wait_recv()
        for q in A.pending + B.pending:
            q.wait_send()
        wait_bytes(xb.at[pl.ds(0, 240), :], 0, True)
        wait_bytes(rs16, 1, True)
        wait_bytes(rs32, 2, True)
        wait_bytes(ga.at[pl.ds(0, 32 - PW)], 3, True)
        wait_bytes(gall.at[pl.ds(0, 15)], 4, True)
        ex.wait_send()
        wait_bytes(prs, 6, True)
        wait_bytes(psum.at[pl.ds(0, 128 - PZ), :], 7, True)
        back.wait_send()
    f32 = jnp.float32
    V = pl.BlockSpec(memory_space=pltpu.VMEM)
    def call(panel, trail):
        return pl.pallas_call(kernel,
            out_shape=[jax.ShapeDtypeStruct((256, K), f32), jax.ShapeDtypeStruct((256, 128), f32), jax.ShapeDtypeStruct((256, 256), f32)],
            in_specs=[pl.BlockSpec(memory_space=pl.ANY), V], out_specs=[V, V, V],
            scratch_shapes=[pltpu.SemaphoreType.DMA((2, NMSG)), pltpu.SemaphoreType.DMA((2, NMSG)), pltpu.SemaphoreType.DMA((2,)),
                pltpu.VMEM((256, 256), f32), pltpu.VMEM((256, 256), f32), pltpu.VMEM((15, 16, 256), f32),
                pltpu.VMEM((32, 1, 128), f32), pltpu.VMEM((PW * (NR - 1), 1, 128), f32), pltpu.VMEM((32, 1, 128), f32), pltpu.VMEM((16, 32, 1, 128), f32),
                pltpu.VMEM((256, 128), f32), pltpu.VMEM((128, 128), f32), pltpu.VMEM((PZ * (NZ - 1), 128), f32), pltpu.VMEM((8, 128), f32),
                pltpu.SemaphoreType.DMA((9,)), pltpu.SemaphoreType.DMA((9,))],
            compiler_params=pltpu.CompilerParams(collective_id=0, has_side_effects=True, vmem_limit_bytes=50 << 20))(panel, trail)
    return call

T = 8
N = 128

def factor_half(tiles):
    n = len(tiles)
    sub = lax.broadcasted_iota(jnp.int32, (T, N), 0)
    lane = lax.broadcasted_iota(jnp.int32, (T, N), 1)
    bl = lambda x, c: jnp.broadcast_to(x[:, c:c + 1], (T, N))
    bs = lambda x, r: jnp.broadcast_to(x[r:r + 1, :], (T, N))
    tiles = list(tiles)
    Rs, Ls = [], []
    for k in range(n):
        t = tiles[k]
        inb = (lane >= T * k) & (lane < T * k + T)
        eye = jnp.where(lane - T * k == sub, 1.0, 0.0)
        cols = [bl(t, T * k + m) for m in range(T)]
        z = jnp.where(inb, eye, t)
        u = t
        li = z
        dinv = jnp.zeros((T, N), jnp.float32)
        drs = jnp.zeros((T, N), jnp.float32)
        for j in range(T):
            piv = bs(cols[j], j)
            r = 1.0 / piv
            f = jnp.where(sub == j, 0.0, cols[j] * r)
            fl = jnp.where(sub > j, f, 0.0)
            for m in range(j + 1, T):
                cols[m] = cols[m] - f * bs(cols[m], j)
            dinv = jnp.where(sub == j, r, dinv)
            drs = jnp.where(sub == j, lax.rsqrt(piv), drs)
            z = z - f * bs(z, j)
            u = u - fl * bs(u, j)
            li = li - fl * bs(li, j)
        z = z * dinv
        row = sub + T * k
        Rs.append(jnp.where(lane >= row, u * drs, 0.0))
        Ls.append(jnp.where(lane <= row, li * drs, 0.0))
        zr = [bs(z, m) for m in range(T)]
        for i in range(k + 1, n):
            ti = tiles[i]
            c = [bl(ti, T * k + m) for m in range(T)]
            p = [c[m] * zr[m] for m in range(T)]
            while len(p) > 1:
                p = [p[a] + p[a + 1] for a in range(0, len(p), 2)]
            tiles[i] = jnp.where(inb, 0.0, ti) - p[0]
    return Rs, Ls


CH = 512
def finish(gram, psum, g, trail, r_ref, top_ref, out, li_ref):
    h = N
    def half(read, ro):
        R, L = factor_half([read(i) for i in range(16)])
        for i in range(16):
            r_ref[ro + 8 * i: ro + 8 * i + 8, ro:ro + h] = R[i]
            li_ref[ro + 8 * i: ro + 8 * i + 8, ro:ro + h] = L[i]
    @pl.when(pl.program_id(0) == 0)
    def _():
        half(lambda i: gram[8 * i:8 * i + 8, :h], 0)
        linv1 = li_ref[:h, :h]
        r12 = dot(linv1, gram[:h, h:])
        r_ref[:h, h:] = r12
        r_ref[h:, :h] = jnp.zeros((h, h), jnp.float32)
        li_ref[:h, h:] = jnp.zeros((h, h), jnp.float32)
        s = gram[h:, h:] - dot(r12, r12, 0, 0)
        half(lambda i: s[8 * i:8 * i + 8, :], h)
        t = dot(r12, linv1, 0, 0)
        li_ref[h:, :h] = -dot(li_ref[h:, h:], t)
        top_ref[...] = dot(li_ref[...], psum[...])
        psum[...] = dot(li_ref[...], top_ref[...], 0, 0)
    out[...] = trail[...] - dot(g[...], psum[...], 0, 0)

def finish_call(gram, psum, g, trail):
    f32 = jnp.float32
    W = lambda s: pl.BlockSpec(s, lambda i: (0, 0))
    def kk(gram, psum_in, g, trail, r_ref, top_ref, out, li_ref, cf):
        @pl.when(pl.program_id(0) == 0)
        def _():
            cf[...] = psum_in[...]
        finish(gram, cf, g, trail, r_ref, top_ref, out, li_ref)
    return pl.pallas_call(kk, grid=(K // CH,),
        in_specs=[W((256, 256)), W((256, 128)), pl.BlockSpec((256, CH), lambda i: (0, i)), pl.BlockSpec((CH, 128), lambda i: (i, 0))],
        out_specs=[W((256, 256)), W((256, 128)), pl.BlockSpec((CH, 128), lambda i: (i, 0))],
        out_shape=[jax.ShapeDtypeStruct((256, 256), f32), jax.ShapeDtypeStruct((256, 128), f32), jax.ShapeDtypeStruct((K, 128), f32)],
        scratch_shapes=[pltpu.VMEM((256, 256), f32), pltpu.VMEM((256, 128), f32)],
        compiler_params=pltpu.CompilerParams(vmem_limit_bytes=40 << 20))(gram, psum, g, trail)

def solution(mesh):
    k=make_kernel(mesh.shape["row"])
    def body(panel, trail):
        g, ps, gram = k(panel, trail)
        return tuple(finish_call(gram, ps, g, trail))
    return jax.shard_map(body, mesh=mesh, in_specs=(P("col","row"),P("row","col")), out_specs=(P(),P(None,"col"),P("row","col")), check_vma=False)
```

time: 1450 us -> 108 us (0.07)
  other arithmetic: 1110 us -> 0 us
  waiting for transfers between devices: 148 us -> 0 us
  matrix products: 106 us -> 0 us
  Pallas kernels: 0 us -> 102 us
  loops' own time: 39.9 us -> 0 us
  local copies, waits for them, and re-layouts: 30.7 us -> 4.71 us
  between operations: 15.2 us -> 0.66 us
    another operation x196 -> x0, other arithmetic: 1110 us -> none  [the longest x186 1050 us: stacked_factor(): return jnp.linalg.cholesky(joined).T]
    all_gather x2 -> x0, waiting for transfers between devices: 147 us -> none  [the longest x1 75.2 us: body(): gathered = lax.all_gather(panel_t, 'col', axis=0, tiled=True)]
    pallas_call x0 -> x2, Pallas kernels: none -> 102 us  [the longest x1 84.8 us: call(): pl.pallas_call(kernel, out_shape=[jax.ShapeDtypeStruct((256, K), f32), ja...]
    dot_general x65 -> x0, matrix products: 87.4 us -> none  [the longest x31 50.7 us: stacked_factor(): lax.dot_general(second_factor, second_factor, (((0,), (0,)), ((), ())), p...]
    another operation x2 -> x0, loops' own time: 39.9 us -> none  [the longest x1 39.9 us: merged(): lax.scan(lambda subtotal, slab: (join(subtotal, slab), None), head, tail)]
    another operation x70 -> x0, matrix products: 18.2 us -> none  [the longest x62 14.6 us: stacked_factor(): return jnp.linalg.cholesky(joined).T]
    slice x4 -> x0, local copies, waits for them, and re-layouts: 15.9 us -> none  [the longest x2 15.9 us: merged(): tail = pieces[1:]]
  transfers between devices with their start and end apart: 3 -> 0, of which waited for: 2 -> 0; matrix products, arithmetic and copies ran while one was open for 82% -> 0% of each run, Pallas kernels for 0% -> 0%
where the time goes in v1:
time: 108 us; the launch traced here: 107 us
  Pallas kernels  102 us (94%)
  local copies, waits for them, and re-layouts  4.71 us (4%)
    pallas_call x1, Pallas kernels, call(): pl.pallas_call(kernel, out_shape=[jax.ShapeDtypeStruct((256, K), f32), ja...  84.8 us
    pallas_call x1, Pallas kernels, finish_call(): pl.pallas_call(kk, grid=(K // CH,), in_specs=[W((256, 256)), W((256, 128)...  17.3 us
    unnamed x6, local copies, waits for them, and re-layouts  4.71 us

profile of v1, /device:TPU:1, one launch (start us, length us, event | category | flops | bytes accessed | tf_op | source)
XLA Modules:
  0.0 107.5 jit_solution(3760185123164757464)
XLA Ops:
  0.6 0.0 copy-start
  0.6 1.6 %copy-done = f32[4096,128]{1,0:T(8,128)S(1)} copy-done((f32[4096,128]{1,0:T(8,128)S(1)}, f32[4096,128]{1,0:T(8,128)}, u32[]{:S(2)}) %copy-start) | copy-done | bytes 2097176
  2.2 0.0 copy-start.2
  2.2 0.9 copy-done.2
  3.2 84.8 %shard_map.49 = (f32[256,4096]{1,0:T(8,128)}, f32[256,128]{1,0:T(8,128)S(1)}, f32[256,256]{1,0:T(8,128)S(1)}) custom-call(f32[16,4096]{1,0:T(8,128)S(1)} %copy-done.2, f32[4096,128]{1,0:T(8,128)S(1)} %copy-done), custom_call_target="tpu_custom_call" | custom-call | tf_op jit(solution)/shard_map/pallas_call | solution.py:205
  88.0 0.0 copy-start.1
  88.0 2.2 %copy-done.1 = f32[256,4096]{1,0:T(8,128)S(1)} copy-done((f32[256,4096]{1,0:T(8,128)S(1)}, f32[256,4096]{1,0:T(8,128)}, u32[]{:S(2)}) %copy-start.1) | copy-done | bytes 4194328
  90.2 17.3 %shard_map.50 = (f32[256,256]{1,0:T(8,128)}, f32[256,128]{1,0:T(8,128)}, f32[4096,128]{1,0:T(8,128)}) custom-call(f32[256,256]{1,0:T(8,128)S(1)} %get-tuple-element.6.gram, f32[256,128]{1,0:T(8,128)S(1)} %get-tuple-element.7.psum_in, f32[256,4096]{1,0:T(8,128)S(1)} %copy-done.1, f32[4096,128]{1,0:T(8,128)S(1)} %copy-done), custom_call_target="tpu_custom_call" | custom-call | tf_op jit(solution)/shard_map/pallas_call | solution.py:296
Async XLA Ops:
  0.6 1.6 %copy-start = (f32[4096,128]{1,0:T(8,128)S(1)}, f32[4096,128]{1,0:T(8,128)}, u32[]{:S(2)}) copy-start(f32[4096,128]{1,0:T(8,128)} %trail.3) | copy-start | bytes 6291460
  2.2 0.9 copy-start.2
  88.0 2.2 %copy-start.1 = (f32[256,4096]{1,0:T(8,128)S(1)}, f32[256,4096]{1,0:T(8,128)}, u32[]{:S(2)}) copy-start(f32[256,4096]{1,0:T(8,128)} %get-tuple-element.8.g) | copy-start | bytes 12582916

commit v2 on v1

v2 whole, which is shorter than its diff:
```python
import jax
import jax.numpy as jnp
from jax import lax
from jax.experimental import pallas as pl
from jax.experimental.pallas import tpu as pltpu
from jax.sharding import PartitionSpec as P

MESH = pl.DeviceIdType.MESH
K = 4096
H = K // 2
S1P, S1M, F1P, F1M = 0, 1, 2, 3
S2P, S2M, F2P, F2M = 4, 9, 14, 18
NMSG = 22

class Half:
    def __init__(self, half, panel, g, ssem, rsem, x, y):
        self.h, self.panel, self.g, self.ss, self.rs = half, panel, g, ssem, rsem
        self.p, self.q = (x, y) if half == 0 else (y, x)
        w = lambda v: lax.rem(v, 4)
        self.P = [self.p, w(self.p + 3), w(self.p + 1), w(self.p + 2)]
        self.Q = [self.q, w(self.q + 3), w(self.q + 1), w(self.q + 2)]
        self.pending = []
    def col(self, p, q):
        return p * 4 + q if self.h == 0 else q * 4 + p
    def slc(self, p, q, lo, n):
        r = pl.multiple_of(self.col(p, q) * 16 + 8 * self.h, 8)
        return self.g.at[pl.ds(r, 8), pl.ds(lo, n)]
    def send(self, m, p, q, lo, n, axis, sign, own=False):
        dst = self.slc(p, q, lo, n)
        src = self.panel.at[pl.ds(8 * self.h, 8), pl.ds(lo, n)] if own else dst
        i = 1 if sign < 0 else 2
        to = self.col(self.P[i], self.q) if axis == 1 else self.col(self.p, self.Q[i])
        c = pltpu.make_async_remote_copy(src, dst, self.ss.at[self.h, m], self.rs.at[self.h, m], device_id={"col": to}, device_id_type=MESH)
        c.start()
        self.pending.append(c)
    def recv(self, m, p, q, lo, n):
        d = self.slc(p, q, lo, n)
        pltpu.make_async_remote_copy(d, d, self.ss.at[self.h, m], self.rs.at[self.h, m], device_id={"col": self.col(self.P[1], self.q)}, device_id_type=MESH).wait_recv()
    def start_own(self):
        self.send(S1P, self.p, self.q, 0, K, 1, 1, True)
        self.send(S1M, self.p, self.q, 0, K, 1, -1, True)
    def start_own2(self):
        self.send(S2P, self.p, self.q, 0, K, 2, 1, True)
        self.send(S2M, self.p, self.q, 0, K, 2, -1, True)
    def first_p(self):
        pm = self.P[1]
        self.recv(S1P, pm, self.q, 0, K)
        self.send(F1P, pm, self.q, 0, H, 1, 1)
        self.send(S2P + 1, pm, self.q, 0, K, 2, 1)
        self.send(S2M + 1, pm, self.q, 0, K, 2, -1)
    def first_m(self):
        pp = self.P[2]
        self.recv(S1M, pp, self.q, 0, K)
        self.send(F1M, pp, self.q, H, H, 1, -1)
        self.send(S2P + 2, pp, self.q, 0, K, 2, 1)
        self.send(S2M + 2, pp, self.q, 0, K, 2, -1)
    def far(self):
        po = self.P[3]
        self.recv(F1P, po, self.q, 0, H)
        self.send(S2P + 3, po, self.q, 0, H, 2, 1)
        self.send(S2M + 3, po, self.q, 0, H, 2, -1)
        self.recv(F1M, po, self.q, H, H)
        self.send(S2P + 4, po, self.q, H, H, 2, 1)
        self.send(S2M + 4, po, self.q, H, H, 2, -1)
    def second(self, s):
        ps = self.P[s]
        if s < 3:
            self.recv(S2P + s, ps, self.Q[1], 0, K)
            self.send(F2P + s, ps, self.Q[1], 0, H, 2, 1)
            self.recv(S2M + s, ps, self.Q[2], 0, K)
            self.send(F2M + s, ps, self.Q[2], H, H, 2, -1)
        else:
            self.recv(S2P + 3, ps, self.Q[1], 0, H)
            self.send(F2P + 3, ps, self.Q[1], 0, H, 2, 1)
            self.recv(S2M + 3, ps, self.Q[2], 0, H)
            self.recv(S2P + 4, ps, self.Q[1], H, H)
            self.recv(S2M + 4, ps, self.Q[2], H, H)
            self.send(F2M + 3, ps, self.Q[2], H, H, 2, -1)
    def last(self, s):
        ps, qo = self.P[s], self.Q[3]
        self.recv(F2P + s, ps, qo, 0, H)
        self.recv(F2M + s, ps, qo, H, H)


HI = lax.Precision.HIGHEST
T = 8
N = 128

def dot(a, b, ca=1, cb=0):
    return lax.dot_general(a, b, (((ca,), (cb,)), ((), ())), precision=HI, preferred_element_type=jnp.float32)

def factor_half(tiles):
    n = len(tiles)
    sub = lax.broadcasted_iota(jnp.int32, (T, N), 0)
    lane = lax.broadcasted_iota(jnp.int32, (T, N), 1)
    bl = lambda x, c: jnp.broadcast_to(x[:, c:c + 1], (T, N))
    bs = lambda x, r: jnp.broadcast_to(x[r:r + 1, :], (T, N))
    tiles = list(tiles)
    Rs, Ls = [], []
    for k in range(n):
        t = tiles[k]
        inb = (lane >= T * k) & (lane < T * k + T)
        eye = jnp.where(lane - T * k == sub, 1.0, 0.0)
        cols = [bl(t, T * k + m) for m in range(T)]
        z = jnp.where(inb, eye, t)
        u = t
        li = z
        dinv = jnp.zeros((T, N), jnp.float32)
        drs = jnp.zeros((T, N), jnp.float32)
        for j in range(T):
            piv = bs(cols[j], j)
            r = 1.0 / piv
            f = jnp.where(sub == j, 0.0, cols[j] * r)
            fl = jnp.where(sub > j, f, 0.0)
            for m in range(j + 1, T):
                cols[m] = cols[m] - f * bs(cols[m], j)
            dinv = jnp.where(sub == j, r, dinv)
            drs = jnp.where(sub == j, lax.rsqrt(piv), drs)
            z = z - f * bs(z, j)
            u = u - fl * bs(u, j)
            li = li - fl * bs(li, j)
        z = z * dinv
        row = sub + T * k
        Rs.append(jnp.where(lane >= row, u * drs, 0.0))
        Ls.append(jnp.where(lane <= row, li * drs, 0.0))
        zr = [bs(z, m) for m in range(T)]
        for i in range(k + 1, n):
            ti = tiles[i]
            c = [bl(ti, T * k + m) for m in range(T)]
            p = [c[m] * zr[m] for m in range(T)]
            while len(p) > 1:
                p = [p[a] + p[a + 1] for a in range(0, len(p), 2)]
            tiles[i] = jnp.where(inb, 0.0, ti) - p[0]
    return Rs, Ls


NC = 16
F32 = jnp.float32
BF = jnp.bfloat16
FULL = "agpc"

def make_kernel(NR, parts=FULL):
    NZ = NR // 2
    WITH_A, WITH_G, WITH_P, WITH_C = (k in parts for k in "agpc")
    def kernel(panel, trail, g_out, psum, r_out, li_out,
               g, ssem, rsem, lsem, xb, tr, t2, gp3, gx, rs16, zb, gall, pp, px, prs, pall, qs, qr):
        c = lax.axis_index("col")
        w = lax.axis_index("row")
        x, y = c // 4, lax.rem(c, 4)
        z, core = w // 2, lax.rem(w, 2)
        sib = {"row": z * 2 + 1 - core}
        cols = [lax.rem(c + i, NC) for i in range(1, NC)]
        zs = [lax.rem(z + i, NZ) for i in range(1, NZ)]
        own = pltpu.make_async_copy(panel, g.at[pl.ds(pl.multiple_of(c * 16, 16), 16), :], lsem.at[0])
        own.start()
        mine = pltpu.make_async_copy(panel.at[:, pl.ds(pl.multiple_of(c * 256, 256), 256)], xb.at[pl.ds(pl.multiple_of(c * 16, 16), 16), :], lsem.at[1])
        mine.start()
        tcopy = pltpu.make_async_copy(trail, tr, lsem.at[2])
        tcopy.start()
        A = Half(0, panel, g, ssem, rsem, x, y)
        B = Half(1, panel, g, ssem, rsem, x, y)
        bar = pltpu.get_barrier_semaphore()
        for i in range(1, NR):
            pl.semaphore_signal(bar, inc=1, device_id={"row": lax.rem(w + i, NR)}, device_id_type=MESH)
        for j in cols:
            pl.semaphore_signal(bar, inc=1, device_id={"col": j}, device_id_type=MESH)
        pl.semaphore_wait(bar, NC + NR - 2)

        def send(k, src, dst, dev):
            pltpu.make_async_remote_copy(src, dst, qs.at[k], qr.at[k], device_id=dev, device_id_type=MESH).start()
        def got(k, ref, sent=False):
            d = pltpu.make_async_remote_copy(ref, ref, qs.at[k], qr.at[k], device_id=sib, device_id_type=MESH)
            d.wait_send() if sent else d.wait_recv()

        def g_rows():
            for j in cols:
                send(0, panel.at[:, pl.ds(pl.multiple_of(j * 256, 256), 256)], xb.at[pl.ds(pl.multiple_of(c * 16, 16), 16), :], {"col": j})
        def g_local():
            mine.wait()
            got(0, xb.at[pl.ds(0, 240), :])
            hi = xb[:128, :]
            xv = xb[...]
            top = dot(hi, xv, 1, 1)
            low = dot(xb[128:, :], xb[128:, :], 1, 1)
            gp3[pl.ds(0, 128), 0, :] = top[:, :128]
            gp3[pl.ds(128, 128), 0, :] = top[:, 128:]
            gp3[pl.ds(256, 128), 0, :] = low
            send(1, gp3.at[pl.ds((1 - core) * 192, 192)], gx, sib)
        def g_pair():
            got(1, gx)
            gx[...] += gp3[pl.ds(core * 192, 192)]
            for i, j in enumerate(cols):
                send(2, gx.at[pl.ds(j * 12, 12)], rs16.at[pl.ds(i * 12, 12)], {"col": j})
        def g_plane():
            got(2, rs16)
            acc = gx[pl.ds(c * 12, 12)]
            for i in range(NC - 1):
                acc = acc + rs16[pl.ds(i * 12, 12)]
            zb[pl.ds(z * 12, 12)] = acc
            for j in zs:
                send(3, zb.at[pl.ds(z * 12, 12)], zb.at[pl.ds(z * 12, 12)], {"row": j * 2 + core})
        def g_all():
            got(3, zb.at[pl.ds(0, 12 * (NZ - 1))])
            acc = zb[pl.ds(0, 12)]
            for i in range(1, NZ):
                acc = acc + zb[pl.ds(i * 12, 12)]
            at = pl.ds(core * 192 + c * 12, 12)
            gall[at] = acc
            for j in cols:
                send(4, gall.at[at], gall.at[at], {"col": j})
        def g_cols():
            got(4, gall.at[pl.ds(0, 180)])
            at = pl.ds(core * 192, 192)
            send(5, gall.at[at], gall.at[at], sib)
        def g_done():
            got(5, gall.at[pl.ds(0, 192)])

        def rows_of(s):
            a = [16 * A.col(A.P[s], q) for q in range(4)]
            b = [16 * B.col(B.P[s], q) + 8 for q in range(4)]
            return [pl.multiple_of(v, 8) for v in a + b]
        CH = 512
        def p_local(lo, n):
            rows = [r for s in range(lo, lo + n) for r in rows_of(s)]
            m = 64 * n
            def step(i, acc):
                k0 = pl.multiple_of(i * CH, CH)
                v = jnp.concatenate([g[pl.ds(r, 8), pl.ds(k0, CH)] for r in rows], axis=0)
                hi = v.astype(BF)
                l = (v - hi.astype(F32)).astype(BF)
                return acc + jnp.dot(jnp.concatenate([hi, l], axis=0), t2[pl.ds(k0, CH), :], preferred_element_type=F32)
            acc = lax.fori_loop(0, K // CH, step, jnp.zeros((2 * m, 256), F32))
            v = (acc[:m, 128:] + acc[m:, 128:]) + acc[m:, :128] + acc[:m, :128]
            pp[pl.ds(64 * lo, m), 0, :] = v
        def p_pair(k, lo, n):
            h = 32 * n
            send(k, pp.at[pl.ds(64 * lo + (1 - core) * h, h)], px.at[pl.ds(32 * lo, h)], sib)
        def p_scatter(k, lo, n):
            h = 32 * n; u = h // NZ
            got(k, px.at[pl.ds(0, h)])
            at = pl.ds(32 * lo, h)
            px[at] += pp[pl.ds(64 * lo + core * h, h)]
            for i, j in enumerate(zs):
                send(k + 1, px.at[pl.ds(32 * lo + j * u, u)], prs.at[pl.ds((NZ - 1) * (32 // NZ) * lo + i * u, u)], {"row": j * 2 + core})
        def p_spread(k, lo, n):
            h = 32 * n; u = h // NZ
            got(k + 1, prs.at[pl.ds(0, (NZ - 1) * u)])
            acc = px[pl.ds(32 * lo + z * u, u)]
            for i in range(NZ - 1):
                acc = acc + prs[pl.ds((NZ - 1) * (32 // NZ) * lo + i * u, u)]
            at = pl.ds(64 * lo + core * h + z * u, u)
            pall[at] = acc
            for j in zs:
                send(k + 2, pall.at[at], pall.at[at], {"row": j * 2 + core})
        def p_back(k, lo, n):
            h = 32 * n; u = h // NZ
            got(k + 2, pall.at[pl.ds(0, (NZ - 1) * u)])
            at = pl.ds(64 * lo + core * h, h)
            send(k + 3, pall.at[at], pall.at[at], sib)
        def p_done(k, lo, n):
            got(k + 3, pall.at[pl.ds(0, 32 * n)])
            for s in range(lo, lo + n):
                for t, r in enumerate(rows_of(s)):
                    psum[pl.ds(r, 8), :] = pall[pl.ds(64 * s + 8 * t, 8), 0, :]
        def p_sent(k, n):
            h = 32 * n; u = h // NZ
            got(k, px.at[pl.ds(0, h)], True)
            got(k + 1, prs.at[pl.ds(0, (NZ - 1) * u)], True)
            got(k + 2, pall.at[pl.ds(0, (NZ - 1) * u)], True)
            got(k + 3, pall.at[pl.ds(0, h)], True)

        def f_half(read, o):
            R, L = factor_half([read(i) for i in range(16)])
            for i in range(16):
                r_out[o + 8 * i:o + 8 * i + 8, o:o + 128] = R[i]
                li_out[o + 8 * i:o + 8 * i + 8, o:o + 128] = L[i]
        def f_first():
            f_half(lambda i: gall[pl.ds(8 * i, 8), 0, :], 0)
        def f_second():
            linv1 = li_out[:128, :128]
            r12 = dot(linv1, gall[pl.ds(128, 128), 0, :])
            r_out[:128, 128:] = r12
            r_out[128:, :128] = jnp.zeros((128, 128), F32)
            li_out[:128, 128:] = jnp.zeros((128, 128), F32)
            s = gall[pl.ds(256, 128), 0, :] - dot(r12, r12, 0, 0)
            f_half(lambda i: s[8 * i:8 * i + 8, :], 128)
            li_out[128:, :128] = -dot(li_out[128:, 128:], dot(r12, linv1, 0, 0))
        def split_trail():
            tcopy.wait()
            @pl.loop(0, K // CH)
            def _(i):
                at = pl.ds(pl.multiple_of(i * CH, CH), CH)
                v = tr[at, :]
                hi = v.astype(BF)
                t2[at, :128] = hi
                t2[at, 128:] = (v - hi.astype(F32)).astype(BF)

        def G(f, *a):
            if WITH_G: f(*a)
        def GA(*names):
            if WITH_A:
                for nm in names:
                    nm, *a = nm if isinstance(nm, tuple) else (nm,)
                    getattr(A, nm)(*a); getattr(B, nm)(*a)
        def PR(f, *a):
            if WITH_P: f(*a)
        G(g_rows)
        GA("start_own")
        split_trail()
        G(g_local)
        G(g_pair)
        GA("start_own2", "first_p", "first_m")
        G(g_plane)
        GA(("second", 0), "far", ("second", 1), ("second", 2))
        G(g_all)
        GA(("second", 3), ("last", 0), ("last", 1), ("last", 2))
        own.wait()
        PR(p_local, 0, 3)
        PR(p_pair, 6, 0, 3)
        G(g_cols)
        PR(p_scatter, 6, 0, 3)
        G(g_done)
        GA(("last", 3))
        gcopy = pltpu.make_async_copy(g, g_out, lsem.at[3])
        gcopy.start()
        PR(p_local, 3, 1)
        PR(p_pair, 10, 3, 1)
        if WITH_C: f_first()
        PR(p_spread, 6, 0, 3)
        PR(p_scatter, 10, 3, 1)
        if WITH_C: f_second()
        PR(p_back, 6, 0, 3)
        PR(p_spread, 10, 3, 1)
        PR(p_done, 6, 0, 3)
        PR(p_back, 10, 3, 1)
        PR(p_done, 10, 3, 1)
        gcopy.wait()
        if not WITH_G:
            mine.wait()
        for q in A.pending + B.pending:
            q.wait_send()
        if WITH_G:
            got(0, xb.at[pl.ds(0, 240), :], True)
            got(1, gx, True)
            got(2, rs16, True)
            got(3, zb.at[pl.ds(0, 12 * (NZ - 1))], True)
            got(4, gall.at[pl.ds(0, 180)], True)
            got(5, gall.at[pl.ds(0, 192)], True)
        PR(p_sent, 6, 3)
        PR(p_sent, 10, 1)
    V = pl.BlockSpec(memory_space=pltpu.VMEM)
    HB = pl.BlockSpec(memory_space=pltpu.HBM)
    def call(panel, trail):
        sh = lambda *s: jax.ShapeDtypeStruct(s, F32)
        vm = lambda *s: pltpu.VMEM(s, F32)
        return pl.pallas_call(kernel,
            out_shape=[sh(256, K), sh(256, 128), sh(256, 256), sh(256, 256)],
            in_specs=[HB, HB], out_specs=[HB, V, V, V],
            scratch_shapes=[vm(256, K), pltpu.SemaphoreType.DMA((2, NMSG)), pltpu.SemaphoreType.DMA((2, NMSG)), pltpu.SemaphoreType.DMA((4,)),
                vm(256, 256), vm(K, 128), pltpu.VMEM((K, 256), BF),
                vm(384, 1, 128), vm(192, 1, 128), vm(180, 1, 128), vm(12 * NZ, 1, 128), vm(384, 1, 128),
                vm(256, 1, 128), vm(128, 1, 128), vm(128 * (NZ - 1) // NZ, 1, 128), vm(256, 1, 128),
                pltpu.SemaphoreType.DMA((14,)), pltpu.SemaphoreType.DMA((14,))],
            compiler_params=pltpu.CompilerParams(collective_id=0, has_side_effects=True, vmem_limit_bytes=60 << 20))(panel, trail)
    return call

UC = 512
F32 = jnp.float32
def finish(psum, r_in, li, g, trail, r_out, top, out, cf):
    @pl.when(pl.program_id(0) == 0)
    def _():
        r_out[...] = r_in[...]
        t = dot(li[...], psum[...])
        top[...] = t
        cf[...] = dot(li[...], t, 0, 0)
    out[...] = trail[...] - dot(g[...], cf[...], 0, 0)

def finish_call(psum, r_in, li, g, trail):
    V = pl.BlockSpec(memory_space=pltpu.VMEM)
    W = lambda s: pl.BlockSpec(s, lambda i: (0, 0))
    sh = lambda *s: jax.ShapeDtypeStruct(s, F32)
    return pl.pallas_call(finish, grid=(K // UC,),
        in_specs=[W((256, 128)), W((256, 256)), W((256, 256)), pl.BlockSpec((256, UC), lambda i: (0, i)), pl.BlockSpec((UC, 128), lambda i: (i, 0))],
        out_specs=[W((256, 256)), W((256, 128)), pl.BlockSpec((UC, 128), lambda i: (i, 0))],
        out_shape=[sh(256, 256), sh(256, 128), sh(K, 128)],
        scratch_shapes=[pltpu.VMEM((256, 128), F32)],
        compiler_params=pltpu.CompilerParams(vmem_limit_bytes=60 << 20))(psum, r_in, li, g, trail)

def solution(mesh):
    k=make_kernel(mesh.shape["row"])
    def body(panel, trail):
        g, ps, r, li = k(panel, trail)
        return tuple(finish_call(ps, r, li, g, trail))
    return jax.shard_map(body, mesh=mesh, in_specs=(P("col","row"),P("row","col")), out_specs=(P(),P(None,"col"),P("row","col")), check_vma=False)
```

time: 108 us -> 87.2 us (0.81)
  Pallas kernels: 102 us -> 86.2 us
  local copies, waits for them, and re-layouts: 4.71 us -> 0 us
    pallas_call x2, Pallas kernels: 102 us -> 86.2 us  [the longest x1 76.1 us: call(): pl.pallas_call(kernel, out_shape=[sh(256, K), sh(256, 128), sh(256, 256),...]
    unnamed x6 -> x0, local copies, waits for them, and re-layouts: 4.71 us -> none
where the time goes in v2:
time: 87.2 us; the launch traced here: 86.9 us
  Pallas kernels  86.2 us (99%)
    pallas_call x1, Pallas kernels, call(): pl.pallas_call(kernel, out_shape=[sh(256, K), sh(256, 128), sh(256, 256),...  76.1 us
    pallas_call x1, Pallas kernels, finish_call(): pl.pallas_call(finish, grid=(K // UC,), in_specs=[W((256, 128)), W((256,...  10.1 us

profile of v2, /device:TPU:1, one launch (start us, length us, event | category | flops | bytes accessed | tf_op | source)
XLA Modules:
  0.0 86.9 jit_solution(4599681090490304057)
XLA Ops:
  0.6 76.1 %shard_map.49 = (f32[256,4096]{1,0:T(8,128)}, f32[256,128]{1,0:T(8,128)}, f32[256,256]{1,0:T(8,128)}, f32[256,256]{1,0:T(8,128)}) custom-call(f32[16,4096]{1,0:T(8,128)} %panel.1, f32[4096,128]{1,0:T(8,128)} %trail.3), custom_call_target="tpu_custom_call" | custom-call | tf_op jit(solution)/shard_map/pallas_call | solution.py:356
  76.8 10.1 %shard_map.50 = (f32[256,256]{1,0:T(8,128)}, f32[256,128]{1,0:T(8,128)}, f32[4096,128]{1,0:T(8,128)}) custom-call(f32[256,128]{1,0:T(8,128)} %get-tuple-element.7.psum, f32[256,256]{1,0:T(8,128)} %get-tuple-element.8.r_in, f32[256,256]{1,0:T(8,128)} %get-tuple-element.9.li, f32[256,4096]{1,0:T(8,128)} %get-tuple-element.10.g, f32[4096,128]{1,0:T(8,128)} %trail.3), custom_call_target="tpu_custom_call" | custom-call | tf_op jit(solution)/shard_map/pallas_call | solution.py:382

commit v3 on v2

--- a/solution.py
+++ b/solution.py
@@ -89,14 +89,13 @@
 def dot(a, b, ca=1, cb=0):
     return lax.dot_general(a, b, (((ca,), (cb,)), ((), ())), precision=HI, preferred_element_type=jnp.float32)
 
-def factor_half(tiles):
+def factor_steps(tiles, put):
     n = len(tiles)
     sub = lax.broadcasted_iota(jnp.int32, (T, N), 0)
     lane = lax.broadcasted_iota(jnp.int32, (T, N), 1)
     bl = lambda x, c: jnp.broadcast_to(x[:, c:c + 1], (T, N))
     bs = lambda x, r: jnp.broadcast_to(x[r:r + 1, :], (T, N))
     tiles = list(tiles)
-    Rs, Ls = [], []
     for k in range(n):
         t = tiles[k]
         inb = (lane >= T * k) & (lane < T * k + T)
@@ -121,8 +120,7 @@
             li = li - fl * bs(li, j)
         z = z * dinv
         row = sub + T * k
-        Rs.append(jnp.where(lane >= row, u * drs, 0.0))
-        Ls.append(jnp.where(lane <= row, li * drs, 0.0))
+        put(k, jnp.where(lane >= row, u * drs, 0.0), jnp.where(lane <= row, li * drs, 0.0))
         zr = [bs(z, m) for m in range(T)]
         for i in range(k + 1, n):
             ti = tiles[i]
@@ -131,19 +129,34 @@
             while len(p) > 1:
                 p = [p[a] + p[a + 1] for a in range(0, len(p), 2)]
             tiles[i] = jnp.where(inb, 0.0, ti) - p[0]
-    return Rs, Ls
+        yield k
 
 
 NC = 16
 F32 = jnp.float32
 BF = jnp.bfloat16
-FULL = "agpc"
-
-def make_kernel(NR, parts=FULL):
+ORDER = ("gr own sp gl",
+         "gp own2 fp fm",
+         "gpl s0 far s1",
+         "s2 s3 ga l0",
+         "l1 l2 ow p1",
+         "sc1 l3 p2 gc",
+         "sc2 gd f sp1",
+         "f f sp2 f",
+         "f bk1 f f",
+         "f bk2 e1 e2",
+         "up")
+CUT = 192
+LIMIT = 60 << 20
+
+def split(v):
+    hi = v.astype(BF)
+    return hi, (v - hi.astype(F32)).astype(BF)
+
+def make_kernel(NR, order=ORDER):
     NZ = NR // 2
-    WITH_A, WITH_G, WITH_P, WITH_C = (k in parts for k in "agpc")
-    def kernel(panel, trail, g_out, psum, r_out, li_out,
-               g, ssem, rsem, lsem, xb, tr, t2, gp3, gx, rs16, zb, gall, pp, px, prs, pall, qs, qr):
+    def kernel(panel, trail, r_out, top_out, upd,
+               g, li, ssem, rsem, lsem, us, xb, tr, t2, gp3, gx, rs16, zb, gall, pp, px, prs, pall, pn, qs, qr):
         c = lax.axis_index("col")
         w = lax.axis_index("row")
         x, y = c // 4, lax.rem(c, 4)
@@ -215,180 +228,184 @@
         def g_done():
             got(5, gall.at[pl.ds(0, 192)])
 
-        def rows_of(s):
-            a = [16 * A.col(A.P[s], q) for q in range(4)]
-            b = [16 * B.col(B.P[s], q) + 8 for q in range(4)]
-            return [pl.multiple_of(v, 8) for v in a + b]
+        tiles = [(hf, t, q) for t in range(4) for hf in (A, B) for q in range(4)]
+        rows = [pl.multiple_of(16 * hf.col(hf.P[t], hf.Q[q]) + 8 * hf.h, 8) for hf, t, q in tiles]
+        base = (0, CUT, 256)
         CH = 512
-        def p_local(lo, n):
-            rows = [r for s in range(lo, lo + n) for r in rows_of(s)]
-            m = 64 * n
-            def step(i, acc):
-                k0 = pl.multiple_of(i * CH, CH)
-                v = jnp.concatenate([g[pl.ds(r, 8), pl.ds(k0, CH)] for r in rows], axis=0)
-                hi = v.astype(BF)
-                l = (v - hi.astype(F32)).astype(BF)
+        def p_local(i):
+            lo, hi_ = base[i], base[i + 1]
+            m = hi_ - lo
+            mine_ = rows[lo // 8:hi_ // 8]
+            def step(n, acc):
+                k0 = pl.multiple_of(n * CH, CH)
+                v = jnp.concatenate([g[pl.ds(r, 8), pl.ds(k0, CH)] for r in mine_], axis=0)
+                hi, l = split(v)
                 return acc + jnp.dot(jnp.concatenate([hi, l], axis=0), t2[pl.ds(k0, CH), :], preferred_element_type=F32)
             acc = lax.fori_loop(0, K // CH, step, jnp.zeros((2 * m, 256), F32))
-            v = (acc[:m, 128:] + acc[m:, 128:]) + acc[m:, :128] + acc[:m, :128]
-            pp[pl.ds(64 * lo, m), 0, :] = v
-        def p_pair(k, lo, n):
-            h = 32 * n
-            send(k, pp.at[pl.ds(64 * lo + (1 - core) * h, h)], px.at[pl.ds(32 * lo, h)], sib)
-        def p_scatter(k, lo, n):
-            h = 32 * n; u = h // NZ
-            got(k, px.at[pl.ds(0, h)])
-            at = pl.ds(32 * lo, h)
-            px[at] += pp[pl.ds(64 * lo + core * h, h)]
-            for i, j in enumerate(zs):
-                send(k + 1, px.at[pl.ds(32 * lo + j * u, u)], prs.at[pl.ds((NZ - 1) * (32 // NZ) * lo + i * u, u)], {"row": j * 2 + core})
-        def p_spread(k, lo, n):
-            h = 32 * n; u = h // NZ
-            got(k + 1, prs.at[pl.ds(0, (NZ - 1) * u)])
-            acc = px[pl.ds(32 * lo + z * u, u)]
-            for i in range(NZ - 1):
-                acc = acc + prs[pl.ds((NZ - 1) * (32 // NZ) * lo + i * u, u)]
-            at = pl.ds(64 * lo + core * h + z * u, u)
+            pp[pl.ds(lo, m), 0, :] = ((acc[m:, 128:] + acc[:m, 128:]) + acc[m:, :128]) + acc[:m, :128]
+            h = m // 2
+            send(6 + 4 * i, pp.at[pl.ds(lo + (1 - core) * h, h)], px.at[pl.ds(lo // 2, h)], sib)
+        def p_pair(i):
+            lo, h = base[i], (base[i + 1] - base[i]) // 2
+            at = pl.ds(lo // 2, h)
+            got(6 + 4 * i, px.at[at])
+            return at, px[at] + pp[pl.ds(lo + core * h, h)]
+        def sizes(i):
+            h = (base[i + 1] - base[i]) // 2
+            u = h // NZ
+            return base[i], h, u, (NZ - 1) * base[i] // (2 * NZ)
+        def p_scatter(i):
+            lo, h, u, o = sizes(i)
+            at, v = p_pair(i)
+            px[at] = v
+            for n, j in enumerate(zs):
+                send(7 + 4 * i, px.at[pl.ds(lo // 2 + j * u, u)], prs.at[pl.ds(o + n * u, u)], {"row": j * 2 + core})
+        def p_spread(i):
+            lo, h, u, o = sizes(i)
+            got(7 + 4 * i, prs.at[pl.ds(o, (NZ - 1) * u)])
+            acc = px[pl.ds(lo // 2 + z * u, u)]
+            for n in range(NZ - 1):
+                acc = acc + prs[pl.ds(o + n * u, u)]
+            at = pl.ds(lo + core * h + z * u, u)
             pall[at] = acc
             for j in zs:
-                send(k + 2, pall.at[at], pall.at[at], {"row": j * 2 + core})
-        def p_back(k, lo, n):
-            h = 32 * n; u = h // NZ
-            got(k + 2, pall.at[pl.ds(0, (NZ - 1) * u)])
-            at = pl.ds(64 * lo + core * h, h)
-            send(k + 3, pall.at[at], pall.at[at], sib)
-        def p_done(k, lo, n):
-            got(k + 3, pall.at[pl.ds(0, 32 * n)])
-            for s in range(lo, lo + n):
-                for t, r in enumerate(rows_of(s)):
-                    psum[pl.ds(r, 8), :] = pall[pl.ds(64 * s + 8 * t, 8), 0, :]
-        def p_sent(k, n):
-            h = 32 * n; u = h // NZ
-            got(k, px.at[pl.ds(0, h)], True)
-            got(k + 1, prs.at[pl.ds(0, (NZ - 1) * u)], True)
-            got(k + 2, pall.at[pl.ds(0, (NZ - 1) * u)], True)
-            got(k + 3, pall.at[pl.ds(0, h)], True)
-
-        def f_half(read, o):
-            R, L = factor_half([read(i) for i in range(16)])
-            for i in range(16):
-                r_out[o + 8 * i:o + 8 * i + 8, o:o + 128] = R[i]
-                li_out[o + 8 * i:o + 8 * i + 8, o:o + 128] = L[i]
-        def f_first():
-            f_half(lambda i: gall[pl.ds(8 * i, 8), 0, :], 0)
-        def f_second():
-            linv1 = li_out[:128, :128]
+                send(8 + 4 * i, pall.at[at], pall.at[at], {"row": j * 2 + core})
+        def p_back(i):
+            lo, h, u, o = sizes(i)
+            got(8 + 4 * i, pall.at[pl.ds(0, (NZ - 1) * u)])
+            at = pl.ds(lo + core * h, h)
+            send(9 + 4 * i, pall.at[at], pall.at[at], sib)
+        def p_end(i):
+            lo, h, u, o = sizes(i)
+            got(9 + 4 * i, pall.at[pl.ds(0, h)])
+            for t in range(h // 4):
+                pn[pl.ds(rows[lo // 8 + t], 8), :] = pall[pl.ds(lo + 8 * t, 8), 0, :]
+        def p_sent():
+            for i in range(2):
+                lo, h, u, o = sizes(i)
+                got(6 + 4 * i, px.at[pl.ds(0, h)], True)
+                got(7 + 4 * i, prs.at[pl.ds(0, (NZ - 1) * u)], True)
+                got(8 + 4 * i, pall.at[pl.ds(0, (NZ - 1) * u)], True)
+                got(9 + 4 * i, pall.at[pl.ds(0, h)], True)
+
+        def put_at(o):
+            def put(k, rt, lt):
+                r_out[o + 8 * k:o + 8 * k + 8, o:o + 128] = rt
+                li[o + 8 * k:o + 8 * k + 8, o:o + 128] = lt
+            return put
+        def factor():
+            for k in factor_steps([gall[pl.ds(8 * i, 8), 0, :] for i in range(16)], put_at(0)):
+                if k % 4 == 3: yield
+            linv1 = li[:128, :128]
             r12 = dot(linv1, gall[pl.ds(128, 128), 0, :])
             r_out[:128, 128:] = r12
             r_out[128:, :128] = jnp.zeros((128, 128), F32)
-            li_out[:128, 128:] = jnp.zeros((128, 128), F32)
+            li[:128, 128:] = jnp.zeros((128, 128), F32)
             s = gall[pl.ds(256, 128), 0, :] - dot(r12, r12, 0, 0)
-            f_half(lambda i: s[8 * i:8 * i + 8, :], 128)
-            li_out[128:, :128] = -dot(li_out[128:, 128:], dot(r12, linv1, 0, 0))
+            for k in factor_steps([s[8 * i:8 * i + 8, :] for i in range(16)], put_at(128)):
+                if k == 15:
+                    li[128:, :128] = -dot(li[128:, 128:], dot(r12, linv1, 0, 0))
+                    xb[...] = dot(li[...], li[...], 0, 0)
+                if k % 4 == 3: yield
+        steps = factor()
+        def update():
+            p = pn[...]
+            hi, lo = split(dot(p, xb[...], 0, 0))
+            cf = jnp.concatenate([hi, lo], axis=0)
+            top_out[...] = dot(li[...], p)
+            for n in range(K // CH):
+                at = pl.ds(n * CH, CH)
+                hi, lo = split(g[:, at])
+                a = jnp.dot(cf, hi, preferred_element_type=F32)
+                b = jnp.dot(cf, lo, preferred_element_type=F32)
+                v = ((b[128:] + a[128:]) + b[:128]) + a[:128]
+                tr[at, :] -= v.T
+                pltpu.make_async_copy(tr.at[at, :], upd.at[at, :], us.at[n]).start()
+            for n in range(K // CH):
+                at = pl.ds(n * CH, CH)
+                pltpu.make_async_copy(tr.at[at, :], upd.at[at, :], us.at[n]).wait()
         def split_trail():
             tcopy.wait()
             @pl.loop(0, K // CH)
             def _(i):
                 at = pl.ds(pl.multiple_of(i * CH, CH), CH)
-                v = tr[at, :]
-                hi = v.astype(BF)
+                hi, lo = split(tr[at, :])
                 t2[at, :128] = hi
-                t2[at, 128:] = (v - hi.astype(F32)).astype(BF)
-
-        def G(f, *a):
-            if WITH_G: f(*a)
-        def GA(*names):
-            if WITH_A:
-                for nm in names:
-                    nm, *a = nm if isinstance(nm, tuple) else (nm,)
-                    getattr(A, nm)(*a); getattr(B, nm)(*a)
-        def PR(f, *a):
-            if WITH_P: f(*a)
-        G(g_rows)
-        GA("start_own")
-        split_trail()
-        G(g_local)
-        G(g_pair)
-        GA("start_own2", "first_p", "first_m")
-        G(g_plane)
-        GA(("second", 0), "far", ("second", 1), ("second", 2))
-        G(g_all)
-        GA(("second", 3), ("last", 0), ("last", 1), ("last", 2))
-        own.wait()
-        PR(p_local, 0, 3)
-        PR(p_pair, 6, 0, 3)
-        G(g_cols)
-        PR(p_scatter, 6, 0, 3)
-        G(g_done)
-        GA(("last", 3))
-        gcopy = pltpu.make_async_copy(g, g_out, lsem.at[3])
-        gcopy.start()
-        PR(p_local, 3, 1)
-        PR(p_pair, 10, 3, 1)
-        if WITH_C: f_first()
-        PR(p_spread, 6, 0, 3)
-        PR(p_scatter, 10, 3, 1)
-        if WITH_C: f_second()
-        PR(p_back, 6, 0, 3)
-        PR(p_spread, 10, 3, 1)
-        PR(p_done, 6, 0, 3)
-        PR(p_back, 10, 3, 1)
-        PR(p_done, 10, 3, 1)
-        gcopy.wait()
-        if not WITH_G:
+                t2[at, 128:] = lo
+
+        def both(name, *a):
+            for hf in (A, B):
+                getattr(hf, name)(*a)
+        def adv(n):
+            for _ in range(n): next(steps, None)
+        do = {"gr": g_rows, "gl": g_local, "gp": g_pair, "gpl": g_plane, "ga": g_all, "gc": g_cols, "gd": g_done, "sp": split_trail,
+              "own": lambda: both("start_own"), "own2": lambda: both("start_own2"), "fp": lambda: both("first_p"), "fm": lambda: both("first_m"), "far": lambda: both("far"),
+              "s0": lambda: both("second", 0), "s1": lambda: both("second", 1), "s2": lambda: both("second", 2), "s3": lambda: both("second", 3),
+              "l0": lambda: both("last", 0), "l1": lambda: both("last", 1), "l2": lambda: both("last", 2), "l3": lambda: both("last", 3),
+              "p1": lambda: p_local(0), "p2": lambda: p_local(1), "sc1": lambda: p_scatter(0), "sp1": lambda: p_spread(0), "bk1": lambda: p_back(0), "e1": lambda: p_end(0),
+              "sc2": lambda: p_scatter(1), "sp2": lambda: p_spread(1), "bk2": lambda: p_back(1), "e2": lambda: p_end(1),
+              "up": update, "ow": own.wait,
+              "f": lambda: adv(1)}
+        todo = [w for l in order for w in l.split()]
+        for nm in todo:
+            do[nm]()
+        if "gl" not in todo:
             mine.wait()
+        if "ow" not in todo:
+            own.wait()
+        if "sp" not in todo:
+            tcopy.wait()
         for q in A.pending + B.pending:
             q.wait_send()
-        if WITH_G:
+        if "gr" in todo:
             got(0, xb.at[pl.ds(0, 240), :], True)
             got(1, gx, True)
             got(2, rs16, True)
             got(3, zb.at[pl.ds(0, 12 * (NZ - 1))], True)
             got(4, gall.at[pl.ds(0, 180)], True)
             got(5, gall.at[pl.ds(0, 192)], True)
-        PR(p_sent, 6, 3)
-        PR(p_sent, 10, 1)
+        if "p1" in todo:
+            p_sent()
     V = pl.BlockSpec(memory_space=pltpu.VMEM)
     HB = pl.BlockSpec(memory_space=pltpu.HBM)
     def call(panel, trail):
         sh = lambda *s: jax.ShapeDtypeStruct(s, F32)
         vm = lambda *s: pltpu.VMEM(s, F32)
         return pl.pallas_call(kernel,
-            out_shape=[sh(256, K), sh(256, 128), sh(256, 256), sh(256, 256)],
-            in_specs=[HB, HB], out_specs=[HB, V, V, V],
-            scratch_shapes=[vm(256, K), pltpu.SemaphoreType.DMA((2, NMSG)), pltpu.SemaphoreType.DMA((2, NMSG)), pltpu.SemaphoreType.DMA((4,)),
+            out_shape=[sh(256, 256), sh(256, 128), sh(K, 128)],
+            in_specs=[HB, HB], out_specs=[V, V, HB],
+            scratch_shapes=[vm(256, K), vm(256, 256), pltpu.SemaphoreType.DMA((2, NMSG)), pltpu.SemaphoreType.DMA((2, NMSG)), pltpu.SemaphoreType.DMA((3,)), pltpu.SemaphoreType.DMA((8,)),
                 vm(256, 256), vm(K, 128), pltpu.VMEM((K, 256), BF),
                 vm(384, 1, 128), vm(192, 1, 128), vm(180, 1, 128), vm(12 * NZ, 1, 128), vm(384, 1, 128),
-                vm(256, 1, 128), vm(128, 1, 128), vm(128 * (NZ - 1) // NZ, 1, 128), vm(256, 1, 128),
+                vm(256, 1, 128), vm(128, 1, 128), vm(128 * (NZ - 1) // NZ, 1, 128), vm(256, 1, 128), vm(256, 128),
                 pltpu.SemaphoreType.DMA((14,)), pltpu.SemaphoreType.DMA((14,))],
-            compiler_params=pltpu.CompilerParams(collective_id=0, has_side_effects=True, vmem_limit_bytes=60 << 20))(panel, trail)
+            compiler_params=pltpu.CompilerParams(collective_id=0, has_side_effects=True, vmem_limit_bytes=LIMIT))(panel, trail)
     return call
 
-UC = 512
-F32 = jnp.float32
-def finish(psum, r_in, li, g, trail, r_out, top, out, cf):
-    @pl.when(pl.program_id(0) == 0)
-    def _():
-        r_out[...] = r_in[...]
-        t = dot(li[...], psum[...])
-        top[...] = t
-        cf[...] = dot(li[...], t, 0, 0)
-    out[...] = trail[...] - dot(g[...], cf[...], 0, 0)
-
-def finish_call(psum, r_in, li, g, trail):
-    V = pl.BlockSpec(memory_space=pltpu.VMEM)
-    W = lambda s: pl.BlockSpec(s, lambda i: (0, 0))
-    sh = lambda *s: jax.ShapeDtypeStruct(s, F32)
-    return pl.pallas_call(finish, grid=(K // UC,),
-        in_specs=[W((256, 128)), W((256, 256)), W((256, 256)), pl.BlockSpec((256, UC), lambda i: (0, i)), pl.BlockSpec((UC, 128), lambda i: (i, 0))],
-        out_specs=[W((256, 256)), W((256, 128)), pl.BlockSpec((UC, 128), lambda i: (i, 0))],
-        out_shape=[sh(256, 256), sh(256, 128), sh(K, 128)],
-        scratch_shapes=[pltpu.VMEM((256, 128), F32)],
-        compiler_params=pltpu.CompilerParams(vmem_limit_bytes=60 << 20))(psum, r_in, li, g, trail)
+PARTS = (1, 1, 4)
+def deliver(a, b, c, a_out, b_out, c_out, a_buf, b_buf, c_buf, si, so):
+    moves = []
+    for src, buf, dst, parts in ((c, c_buf, c_out, PARTS[2]), (a, a_buf, a_out, PARTS[0]), (b, b_buf, b_out, PARTS[1])):
+        n = src.shape[0] // parts
+        for i in range(parts):
+            at, k = pl.ds(i * n, n), len(moves)
+            moves.append((pltpu.make_async_copy(src.at[at, :], buf.at[at, :], si.at[k]), pltpu.make_async_copy(buf.at[at, :], dst.at[at, :], so.at[k])))
+    for i, _ in moves: i.start()
+    for i, o in moves:
+        i.wait()
+        o.start()
+    for _, o in moves: o.wait()
+
+def deliver_call(*vals):
+    HB = pl.BlockSpec(memory_space=pl.ANY)
+    return pl.pallas_call(deliver, in_specs=[HB] * 3, out_specs=[HB] * 3,
+        out_shape=[jax.ShapeDtypeStruct(v.shape, F32) for v in vals],
+        scratch_shapes=[pltpu.VMEM(v.shape, F32) for v in vals] + [pltpu.SemaphoreType.DMA((sum(PARTS),))] * 2,
+        compiler_params=pltpu.CompilerParams(vmem_limit_bytes=60 << 20))(*vals)
 
 def solution(mesh):
-    k=make_kernel(mesh.shape["row"])
-    def body(panel, trail):
-        g, ps, r, li = k(panel, trail)
-        return tuple(finish_call(ps, r, li, g, trail))
-    return jax.shard_map(body, mesh=mesh, in_specs=(P("col","row"),P("row","col")), out_specs=(P(),P(None,"col"),P("row","col")), check_vma=False)
+    call = make_kernel(mesh.shape["row"])
+    def body(panel, trailing):
+        return tuple(deliver_call(*call(panel, trailing)))
+    return jax.shard_map(body, mesh=mesh, in_specs=(P("col", "row"), P("row", "col")),
+                         out_specs=(P(), P(None, "col"), P("row", "col")), check_vma=False)

time: 87.2 us -> 80.1 us (0.919)
  Pallas kernels: 86.2 us -> 79.3 us
    pallas_call x2, Pallas kernels: 86.2 us -> 79.3 us  [the longest x1 76.7 us: call(): pl.pallas_call(kernel, out_shape=[sh(256, 256), sh(256, 128), sh(K, 128)]...]
where the time goes in v3:
time: 80.1 us; the launch traced here: 80 us
  Pallas kernels  79.3 us (99%)
    pallas_call x1, Pallas kernels, call(): pl.pallas_call(kernel, out_shape=[sh(256, 256), sh(256, 128), sh(K, 128)]...  76.7 us
    pallas_call x1, Pallas kernels, deliver_call(): pl.pallas_call(deliver, in_specs=[HB] * 3, out_specs=[HB] * 3, out_shape=...  2.58 us

profile of v3, /device:TPU:1, one launch (start us, length us, event | category | flops | bytes accessed | tf_op | source)
XLA Modules:
  0.0 80.0 jit_solution(13950243696296063480)
XLA Ops:
  0.6 76.7 %shard_map.49 = (f32[256,256]{1,0:T(8,128)}, f32[256,128]{1,0:T(8,128)}, f32[4096,128]{1,0:T(8,128)}) custom-call(f32[16,4096]{1,0:T(8,128)} %panel.1, f32[4096,128]{1,0:T(8,128)} %trail.1), custom_call_target="tpu_custom_call" | custom-call | tf_op jit(solution)/shard_map/pallas_call | solution.py:374
  77.4 2.6 %shard_map.50 = (f32[256,256]{1,0:T(8,128)}, f32[256,128]{1,0:T(8,128)}, f32[4096,128]{1,0:T(8,128)}) custom-call(f32[256,256]{1,0:T(8,128)} %get-tuple-element.6.a, f32[256,128]{1,0:T(8,128)} %get-tuple-element.7.b, f32[4096,128]{1,0:T(8,128)} %get-tuple-element.8.c), custom_call_target="tpu_custom_call" | custom-call | tf_op jit(solution)/shard_map/pallas_call | solution.py:401

commit v4 on v3

--- a/solution.py
+++ b/solution.py
@@ -83,7 +83,7 @@
 
 
 HI = lax.Precision.HIGHEST
-T = 8
+T = 16
 N = 128
 
 def dot(a, b, ca=1, cb=0):
@@ -106,47 +106,57 @@
         li = z
         dinv = jnp.zeros((T, N), jnp.float32)
         drs = jnp.zeros((T, N), jnp.float32)
+        piv = bs(cols[0], 0)
         for j in range(T):
-            piv = bs(cols[j], j)
             r = 1.0 / piv
-            f = jnp.where(sub == j, 0.0, cols[j] * r)
-            fl = jnp.where(sub > j, f, 0.0)
+            cj = jnp.where(sub == j, 0.0, cols[j])
+            cl = jnp.where(sub > j, cols[j], 0.0)
+            nxt = None
+            if j + 1 < T:
+                nxt = bs(cols[j + 1], j + 1) - (bs(cols[j], j + 1) * bs(cols[j + 1], j)) * r
             for m in range(j + 1, T):
-                cols[m] = cols[m] - f * bs(cols[m], j)
+                cols[m] = cols[m] - (cj * bs(cols[m], j)) * r
             dinv = jnp.where(sub == j, r, dinv)
             drs = jnp.where(sub == j, lax.rsqrt(piv), drs)
-            z = z - f * bs(z, j)
-            u = u - fl * bs(u, j)
-            li = li - fl * bs(li, j)
+            zj = bs(z, j)
+            li = jnp.where(sub == j, zj, li)
+            u = u - (cl * bs(u, j)) * r
+            z = z - (cj * zj) * r
+            piv = nxt
         z = z * dinv
         row = sub + T * k
         put(k, jnp.where(lane >= row, u * drs, 0.0), jnp.where(lane <= row, li * drs, 0.0))
         zr = [bs(z, m) for m in range(T)]
-        for i in range(k + 1, n):
-            ti = tiles[i]
+        if k + 1 < n:
+            ti = tiles[k + 1]
             c = [bl(ti, T * k + m) for m in range(T)]
             p = [c[m] * zr[m] for m in range(T)]
             while len(p) > 1:
                 p = [p[a] + p[a + 1] for a in range(0, len(p), 2)]
-            tiles[i] = jnp.where(inb, 0.0, ti) - p[0]
+            tiles[k + 1] = jnp.where(inb, 0.0, ti) - p[0]
+        if k + 2 < n:
+            low = jnp.concatenate(tiles[k + 2:], axis=0)
+            d = dot(low[:, T * k:T * k + T], z)
+            for i in range(k + 2, n):
+                tiles[i] = jnp.where(inb, 0.0, tiles[i]) - d[T * (i - k - 2):T * (i - k - 1)]
         yield k
 
 
 NC = 16
 F32 = jnp.float32
 BF = jnp.bfloat16
-ORDER = ("gr own sp gl",
-         "gp own2 fp fm",
+ORDER = ("gr own own2 sp",
+         "gl gp fp fm",
          "gpl s0 far s1",
-         "s2 s3 ga l0",
-         "l1 l2 ow p1",
-         "sc1 l3 p2 gc",
-         "sc2 gd f sp1",
-         "f f sp2 f",
-         "f bk1 f f",
+         "s2 ow p1 s3",
+         "ga sc1 l0 l1",
+         "l2 l3 p2 gc",
+         "sc2 gd f f",
+         "sp1 f f sp2",
+         "f f bk1 f",
          "f bk2 e1 e2",
          "up")
-CUT = 192
+CUT = 160
 LIMIT = 60 << 20
 
 def split(v):
@@ -162,8 +172,10 @@
         x, y = c // 4, lax.rem(c, 4)
         z, core = w // 2, lax.rem(w, 2)
         sib = {"row": z * 2 + 1 - core}
-        cols = [lax.rem(c + i, NC) for i in range(1, NC)]
-        zs = [lax.rem(z + i, NZ) for i in range(1, NZ)]
+        far = lambda i, n: min(i, n - i)
+        steps_c = sorted(((a, b) for a in range(4) for b in range(4) if a + b), key=lambda v: -far(v[0], 4) - far(v[1], 4))
+        cols = [lax.rem(x + a, 4) * 4 + lax.rem(y + b, 4) for a, b in steps_c]
+        zs = [lax.rem(z + i, NZ) for i in sorted(range(1, NZ), key=lambda i: -far(i, NZ))]
         own = pltpu.make_async_copy(panel, g.at[pl.ds(pl.multiple_of(c * 16, 16), 16), :], lsem.at[0])
         own.start()
         mine = pltpu.make_async_copy(panel.at[:, pl.ds(pl.multiple_of(c * 256, 256), 256)], xb.at[pl.ds(pl.multiple_of(c * 16, 16), 16), :], lsem.at[1])
@@ -173,8 +185,10 @@
         A = Half(0, panel, g, ssem, rsem, x, y)
         B = Half(1, panel, g, ssem, rsem, x, y)
         bar = pltpu.get_barrier_semaphore()
-        for i in range(1, NR):
-            pl.semaphore_signal(bar, inc=1, device_id={"row": lax.rem(w + i, NR)}, device_id_type=MESH)
+        for j in zs:
+            for k in range(2):
+                pl.semaphore_signal(bar, inc=1, device_id={"row": j * 2 + k}, device_id_type=MESH)
+        pl.semaphore_signal(bar, inc=1, device_id=sib, device_id_type=MESH)
         for j in cols:
             pl.semaphore_signal(bar, inc=1, device_id={"col": j}, device_id_type=MESH)
         pl.semaphore_wait(bar, NC + NR - 2)
@@ -228,7 +242,9 @@
         def g_done():
             got(5, gall.at[pl.ds(0, 192)])
 
-        tiles = [(hf, t, q) for t in range(4) for hf in (A, B) for q in range(4)]
+        early = [(t, q) for t in range(4) for q in range(3) if t < 3 or q == 0]
+        late = [(t, q) for t in range(4) for q in range(4) if (t, q) not in early]
+        tiles = [(hf, t, q) for t, q in early + late for hf in (A, B)]
         rows = [pl.multiple_of(16 * hf.col(hf.P[t], hf.Q[q]) + 8 * hf.h, 8) for hf, t, q in tiles]
         base = (0, CUT, 256)
         CH = 512
@@ -290,23 +306,23 @@
 
         def put_at(o):
             def put(k, rt, lt):
-                r_out[o + 8 * k:o + 8 * k + 8, o:o + 128] = rt
-                li[o + 8 * k:o + 8 * k + 8, o:o + 128] = lt
+                r_out[o + 16 * k:o + 16 * k + 16, o:o + 128] = rt
+                li[o + 16 * k:o + 16 * k + 16, o:o + 128] = lt
             return put
         def factor():
-            for k in factor_steps([gall[pl.ds(8 * i, 8), 0, :] for i in range(16)], put_at(0)):
-                if k % 4 == 3: yield
+            for k in factor_steps([gall[pl.ds(16 * i, 16), 0, :] for i in range(8)], put_at(0)):
+                if k % 2 == 1: yield
             linv1 = li[:128, :128]
             r12 = dot(linv1, gall[pl.ds(128, 128), 0, :])
             r_out[:128, 128:] = r12
             r_out[128:, :128] = jnp.zeros((128, 128), F32)
             li[:128, 128:] = jnp.zeros((128, 128), F32)
             s = gall[pl.ds(256, 128), 0, :] - dot(r12, r12, 0, 0)
-            for k in factor_steps([s[8 * i:8 * i + 8, :] for i in range(16)], put_at(128)):
-                if k == 15:
+            for k in factor_steps([s[16 * i:16 * i + 16, :] for i in range(8)], put_at(128)):
+                if k == 7:
                     li[128:, :128] = -dot(li[128:, 128:], dot(r12, linv1, 0, 0))
                     xb[...] = dot(li[...], li[...], 0, 0)
-                if k % 4 == 3: yield
+                if k % 2 == 1: yield
         steps = factor()
         def update():
             p = pn[...]

time: 80.1 us -> 71.1 us (0.89)
  Pallas kernels: 79.3 us -> 70.3 us
    pallas_call x1, Pallas kernels: 76.7 us -> 67.8 us  [call(): pl.pallas_call(kernel, out_shape=[sh(256, 256), sh(256, 128), sh(K, 128)]...]
where the time goes in v4:
time: 71.1 us; the launch traced here: 71 us
  Pallas kernels  70.3 us (99%)
    pallas_call x1, Pallas kernels, call(): pl.pallas_call(kernel, out_shape=[sh(256, 256), sh(256, 128), sh(K, 128)]...  67.8 us
    pallas_call x1, Pallas kernels, deliver_call(): pl.pallas_call(deliver, in_specs=[HB] * 3, out_specs=[HB] * 3, out_shape=...  2.58 us

profile of v4, /device:TPU:1, one launch (start us, length us, event | category | flops | bytes accessed | tf_op | source)
XLA Modules:
  0.0 71.0 jit_solution(9897685555821931899)
XLA Ops:
  0.6 67.8 %shard_map.49 = (f32[256,256]{1,0:T(8,128)}, f32[256,128]{1,0:T(8,128)}, f32[4096,128]{1,0:T(8,128)}) custom-call(f32[16,4096]{1,0:T(8,128)} %panel.1, f32[4096,128]{1,0:T(8,128)} %trail.1), custom_call_target="tpu_custom_call" | custom-call | tf_op jit(solution)/shard_map/pallas_call | solution.py:390
  68.4 2.6 %shard_map.50 = (f32[256,256]{1,0:T(8,128)}, f32[256,128]{1,0:T(8,128)}, f32[4096,128]{1,0:T(8,128)}) custom-call(f32[256,256]{1,0:T(8,128)} %get-tuple-element.6.a, f32[256,128]{1,0:T(8,128)} %get-tuple-element.7.b, f32[4096,128]{1,0:T(8,128)} %get-tuple-element.8.c), custom_call_target="tpu_custom_call" | custom-call | tf_op jit(solution)/shard_map/pallas_call | solution.py:417

commit v5 on v4

--- a/solution.py
+++ b/solution.py
@@ -152,9 +152,9 @@
          "ga sc1 l0 l1",
          "l2 l3 p2 gc",
          "sc2 gd f f",
-         "sp1 f f sp2",
-         "f f bk1 f",
-         "f bk2 e1 e2",
+         "sp1 sp2 f f",
+         "f bk1 f f",
+         "bk2 f e1 e2",
          "up")
 CUT = 160
 LIMIT = 60 << 20
@@ -166,7 +166,7 @@
 def make_kernel(NR, order=ORDER):
     NZ = NR // 2
     def kernel(panel, trail, r_out, top_out, upd,
-               g, li, ssem, rsem, lsem, us, xb, tr, t2, gp3, gx, rs16, zb, gall, pp, px, prs, pall, pn, qs, qr):
+               g, li, ssem, rsem, lsem, us, xb, tr, t2, gp3, gx, rs16, zb, gall, pp, px, prs, q1, q2, pall, pn, qs, qr):
         c = lax.axis_index("col")
         w = lax.axis_index("row")
         x, y = c // 4, lax.rem(c, 4)
@@ -247,17 +247,17 @@
         tiles = [(hf, t, q) for t, q in early + late for hf in (A, B)]
         rows = [pl.multiple_of(16 * hf.col(hf.P[t], hf.Q[q]) + 8 * hf.h, 8) for hf, t, q in tiles]
         base = (0, CUT, 256)
-        CH = 512
+        CH, PC = 512, 1024
         def p_local(i):
             lo, hi_ = base[i], base[i + 1]
             m = hi_ - lo
             mine_ = rows[lo // 8:hi_ // 8]
             def step(n, acc):
-                k0 = pl.multiple_of(n * CH, CH)
-                v = jnp.concatenate([g[pl.ds(r, 8), pl.ds(k0, CH)] for r in mine_], axis=0)
+                k0 = pl.multiple_of(n * PC, PC)
+                v = jnp.concatenate([g[pl.ds(r, 8), pl.ds(k0, PC)] for r in mine_], axis=0)
                 hi, l = split(v)
-                return acc + jnp.dot(jnp.concatenate([hi, l], axis=0), t2[pl.ds(k0, CH), :], preferred_element_type=F32)
-            acc = lax.fori_loop(0, K // CH, step, jnp.zeros((2 * m, 256), F32))
+                return acc + jnp.dot(jnp.concatenate([hi, l], axis=0), t2[pl.ds(k0, PC), :], preferred_element_type=F32)
+            acc = lax.fori_loop(0, K // PC, step, jnp.zeros((2 * m, 256), F32))
             pp[pl.ds(lo, m), 0, :] = ((acc[m:, 128:] + acc[:m, 128:]) + acc[m:, :128]) + acc[:m, :128]
             h = m // 2
             send(6 + 4 * i, pp.at[pl.ds(lo + (1 - core) * h, h)], px.at[pl.ds(lo // 2, h)], sib)
@@ -270,6 +270,33 @@
             h = (base[i + 1] - base[i]) // 2
             u = h // NZ
             return base[i], h, u, (NZ - 1) * base[i] // (2 * NZ)
+        LH = (256 - CUT) // 2
+        Q = min(4, NZ)
+        NG = NZ // Q
+        zq, zg = lax.rem(z, Q), z // Q
+        def q_near():
+            _, v = p_pair(1)
+            at = pl.ds(zq * LH, LH)
+            q1[at] = v
+            for i in sorted(range(1, Q), key=lambda i: -far(i, Q)):
+                send(11, q1.at[at], q1.at[at], {"row": (zg * Q + lax.rem(zq + i, Q)) * 2 + core})
+        def total(ref, n):
+            acc = ref[pl.ds(0, LH)]
+            for i in range(1, n):
+                acc = acc + ref[pl.ds(i * LH, LH)]
+            return acc
+        def q_far():
+            got(11, q1.at[pl.ds(0, (Q - 1) * LH)])
+            at = pl.ds(zg * LH, LH)
+            q2[at] = total(q1, Q)
+            for i in sorted(range(1, NG), key=lambda i: -far(i, NG)):
+                send(12, q2.at[at], q2.at[at], {"row": (lax.rem(zg + i, NG) * Q + zq) * 2 + core})
+        def q_back():
+            if NG > 1:
+                got(12, q2.at[pl.ds(0, (NG - 1) * LH)])
+            at = pl.ds(CUT + core * LH, LH)
+            pall[at] = total(q2, NG)
+            send(13, pall.at[at], pall.at[at], sib)
         def p_scatter(i):
             lo, h, u, o = sizes(i)
             at, v = p_pair(i)
@@ -297,12 +324,16 @@
             for t in range(h // 4):
                 pn[pl.ds(rows[lo // 8 + t], 8), :] = pall[pl.ds(lo + 8 * t, 8), 0, :]
         def p_sent():
-            for i in range(2):
-                lo, h, u, o = sizes(i)
-                got(6 + 4 * i, px.at[pl.ds(0, h)], True)
-                got(7 + 4 * i, prs.at[pl.ds(0, (NZ - 1) * u)], True)
-                got(8 + 4 * i, pall.at[pl.ds(0, (NZ - 1) * u)], True)
-                got(9 + 4 * i, pall.at[pl.ds(0, h)], True)
+            lo, h, u, o = sizes(0)
+            got(6, px.at[pl.ds(0, h)], True)
+            got(7, prs, True)
+            got(8, pall.at[pl.ds(0, (NZ - 1) * u)], True)
+            got(9, pall.at[pl.ds(0, h)], True)
+            got(10, px.at[pl.ds(0, LH)], True)
+            got(11, q1.at[pl.ds(0, (Q - 1) * LH)], True)
+            if NG > 1:
+                got(12, q2.at[pl.ds(0, (NG - 1) * LH)], True)
+            got(13, pall.at[pl.ds(0, LH)], True)
 
         def put_at(o):
             def put(k, rt, lt):
@@ -359,7 +390,7 @@
               "s0": lambda: both("second", 0), "s1": lambda: both("second", 1), "s2": lambda: both("second", 2), "s3": lambda: both("second", 3),
               "l0": lambda: both("last", 0), "l1": lambda: both("last", 1), "l2": lambda: both("last", 2), "l3": lambda: both("last", 3),
               "p1": lambda: p_local(0), "p2": lambda: p_local(1), "sc1": lambda: p_scatter(0), "sp1": lambda: p_spread(0), "bk1": lambda: p_back(0), "e1": lambda: p_end(0),
-              "sc2": lambda: p_scatter(1), "sp2": lambda: p_spread(1), "bk2": lambda: p_back(1), "e2": lambda: p_end(1),
+              "sc2": q_near, "sp2": q_far, "bk2": q_back, "e2": lambda: p_end(1),
               "up": update, "ow": own.wait,
               "f": lambda: adv(1)}
         todo = [w for l in order for w in l.split()]
@@ -393,7 +424,7 @@
             scratch_shapes=[vm(256, K), vm(256, 256), pltpu.SemaphoreType.DMA((2, NMSG)), pltpu.SemaphoreType.DMA((2, NMSG)), pltpu.SemaphoreType.DMA((3,)), pltpu.SemaphoreType.DMA((8,)),
                 vm(256, 256), vm(K, 128), pltpu.VMEM((K, 256), BF),
                 vm(384, 1, 128), vm(192, 1, 128), vm(180, 1, 128), vm(12 * NZ, 1, 128), vm(384, 1, 128),
-                vm(256, 1, 128), vm(128, 1, 128), vm(128 * (NZ - 1) // NZ, 1, 128), vm(256, 1, 128), vm(256, 128),
+                vm(256, 1, 128), vm(128, 1, 128), vm(CUT // 2 * (NZ - 1) // NZ, 1, 128), vm(128 - CUT // 2 << 2, 1, 128), vm(128 - CUT // 2 << 2, 1, 128), vm(256, 1, 128), vm(256, 128),
                 pltpu.SemaphoreType.DMA((14,)), pltpu.SemaphoreType.DMA((14,))],
             compiler_params=pltpu.CompilerParams(collective_id=0, has_side_effects=True, vmem_limit_bytes=LIMIT))(panel, trail)
     return call

time: 71.1 us -> 69.1 us (0.972)
  Pallas kernels: 70.3 us -> 68.3 us
    pallas_call x1, Pallas kernels: 67.8 us -> 65.7 us  [call(): pl.pallas_call(kernel, out_shape=[sh(256, 256), sh(256, 128), sh(K, 128)]...]
where the time goes in v5:
time: 69.1 us; the launch traced here: 69 us
  Pallas kernels  68.3 us (99%)
    pallas_call x1, Pallas kernels, call(): pl.pallas_call(kernel, out_shape=[sh(256, 256), sh(256, 128), sh(K, 128)]...  65.7 us
    pallas_call x1, Pallas kernels, deliver_call(): pl.pallas_call(deliver, in_specs=[HB] * 3, out_specs=[HB] * 3, out_shape=...  2.58 us

profile of v5, /device:TPU:1, one launch (start us, length us, event | category | flops | bytes accessed | tf_op | source)
XLA Modules:
  0.0 69.0 jit_solution(17318911335373975565)
XLA Ops:
  0.6 65.7 %shard_map.49 = (f32[256,256]{1,0:T(8,128)}, f32[256,128]{1,0:T(8,128)}, f32[4096,128]{1,0:T(8,128)}) custom-call(f32[16,4096]{1,0:T(8,128)} %panel.1, f32[4096,128]{1,0:T(8,128)} %trail.1), custom_call_target="tpu_custom_call" | custom-call | tf_op jit(solution)/shard_map/pallas_call | solution.py:421
  66.4 2.6 %shard_map.50 = (f32[256,256]{1,0:T(8,128)}, f32[256,128]{1,0:T(8,128)}, f32[4096,128]{1,0:T(8,128)}) custom-call(f32[256,256]{1,0:T(8,128)} %get-tuple-element.6.a, f32[256,128]{1,0:T(8,128)} %get-tuple-element.7.b, f32[4096,128]{1,0:T(8,128)} %get-tuple-element.8.c), custom_call_target="tpu_custom_call" | custom-call | tf_op jit(solution)/shard_map/pallas_call | solution.py:448

commit v6 on v5

--- a/solution.py
+++ b/solution.py
@@ -166,7 +166,7 @@
 def make_kernel(NR, order=ORDER):
     NZ = NR // 2
     def kernel(panel, trail, r_out, top_out, upd,
-               g, li, ssem, rsem, lsem, us, xb, tr, t2, gp3, gx, rs16, zb, gall, pp, px, prs, q1, q2, pall, pn, qs, qr):
+               g, li, rv, tv, ssem, rsem, lsem, us, xb, tr, t2, gp3, gx, rs16, zb, gall, pp, px, prs, q1, q2, pall, pn, qs, qr):
         c = lax.axis_index("col")
         w = lax.axis_index("row")
         x, y = c // 4, lax.rem(c, 4)
@@ -337,7 +337,7 @@
 
         def put_at(o):
             def put(k, rt, lt):
-                r_out[o + 16 * k:o + 16 * k + 16, o:o + 128] = rt
+                rv[o + 16 * k:o + 16 * k + 16, o:o + 128] = rt
                 li[o + 16 * k:o + 16 * k + 16, o:o + 128] = lt
             return put
         def factor():
@@ -345,21 +345,22 @@
                 if k % 2 == 1: yield
             linv1 = li[:128, :128]
             r12 = dot(linv1, gall[pl.ds(128, 128), 0, :])
-            r_out[:128, 128:] = r12
-            r_out[128:, :128] = jnp.zeros((128, 128), F32)
+            rv[:128, 128:] = r12
+            rv[128:, :128] = jnp.zeros((128, 128), F32)
             li[:128, 128:] = jnp.zeros((128, 128), F32)
             s = gall[pl.ds(256, 128), 0, :] - dot(r12, r12, 0, 0)
             for k in factor_steps([s[16 * i:16 * i + 16, :] for i in range(8)], put_at(128)):
                 if k == 7:
                     li[128:, :128] = -dot(li[128:, 128:], dot(r12, linv1, 0, 0))
+                    rout.start()
                     xb[...] = dot(li[...], li[...], 0, 0)
                 if k % 2 == 1: yield
+        rout = pltpu.make_async_copy(rv, r_out, lsem.at[3])
         steps = factor()
         def update():
             p = pn[...]
             hi, lo = split(dot(p, xb[...], 0, 0))
             cf = jnp.concatenate([hi, lo], axis=0)
-            top_out[...] = dot(li[...], p)
             for n in range(K // CH):
                 at = pl.ds(n * CH, CH)
                 hi, lo = split(g[:, at])
@@ -368,9 +369,14 @@
                 v = ((b[128:] + a[128:]) + b[:128]) + a[:128]
                 tr[at, :] -= v.T
                 pltpu.make_async_copy(tr.at[at, :], upd.at[at, :], us.at[n]).start()
+            tv[...] = dot(li[...], p)
+            tout = pltpu.make_async_copy(tv, top_out, lsem.at[4])
+            tout.start()
             for n in range(K // CH):
                 at = pl.ds(n * CH, CH)
                 pltpu.make_async_copy(tr.at[at, :], upd.at[at, :], us.at[n]).wait()
+            rout.wait()
+            tout.wait()
         def split_trail():
             tcopy.wait()
             @pl.loop(0, K // CH)
@@ -413,15 +419,14 @@
             got(5, gall.at[pl.ds(0, 192)], True)
         if "p1" in todo:
             p_sent()
-    V = pl.BlockSpec(memory_space=pltpu.VMEM)
     HB = pl.BlockSpec(memory_space=pltpu.HBM)
     def call(panel, trail):
         sh = lambda *s: jax.ShapeDtypeStruct(s, F32)
         vm = lambda *s: pltpu.VMEM(s, F32)
         return pl.pallas_call(kernel,
             out_shape=[sh(256, 256), sh(256, 128), sh(K, 128)],
-            in_specs=[HB, HB], out_specs=[V, V, HB],
-            scratch_shapes=[vm(256, K), vm(256, 256), pltpu.SemaphoreType.DMA((2, NMSG)), pltpu.SemaphoreType.DMA((2, NMSG)), pltpu.SemaphoreType.DMA((3,)), pltpu.SemaphoreType.DMA((8,)),
+            in_specs=[HB, HB], out_specs=[HB, HB, HB],
+            scratch_shapes=[vm(256, K), vm(256, 256), vm(256, 256), vm(256, 128), pltpu.SemaphoreType.DMA((2, NMSG)), pltpu.SemaphoreType.DMA((2, NMSG)), pltpu.SemaphoreType.DMA((5,)), pltpu.SemaphoreType.DMA((8,)),
                 vm(256, 256), vm(K, 128), pltpu.VMEM((K, 256), BF),
                 vm(384, 1, 128), vm(192, 1, 128), vm(180, 1, 128), vm(12 * NZ, 1, 128), vm(384, 1, 128),
                 vm(256, 1, 128), vm(128, 1, 128), vm(CUT // 2 * (NZ - 1) // NZ, 1, 128), vm(128 - CUT // 2 << 2, 1, 128), vm(128 - CUT // 2 << 2, 1, 128), vm(256, 1, 128), vm(256, 128),

time: 69.1 us -> 68.4 us (0.990)
  Pallas kernels: 68.3 us -> 67.6 us
    pallas_call x1, Pallas kernels: 65.7 us -> 65.1 us  [call(): pl.pallas_call(kernel, out_shape=[sh(256, 256), sh(256, 128), sh(K, 128)]...]
where the time goes in v6:
time: 68.4 us; the launch traced here: 68.3 us
  Pallas kernels  67.6 us (99%)
    pallas_call x1, Pallas kernels, call(): pl.pallas_call(kernel, out_shape=[sh(256, 256), sh(256, 128), sh(K, 128)]...  65.1 us
    pallas_call x1, Pallas kernels, deliver_call(): pl.pallas_call(deliver, in_specs=[HB] * 3, out_specs=[HB] * 3, out_shape=...  2.58 us

profile of v6, /device:TPU:1, one launch (start us, length us, event | category | flops | bytes accessed | tf_op | source)
XLA Modules:
  0.0 68.3 jit_solution(4345021079927543028)
XLA Ops:
  0.6 65.1 %shard_map.49 = (f32[256,256]{1,0:T(8,128)}, f32[256,128]{1,0:T(8,128)}, f32[4096,128]{1,0:T(8,128)}) custom-call(f32[16,4096]{1,0:T(8,128)} %panel.1, f32[4096,128]{1,0:T(8,128)} %trail.1), custom_call_target="tpu_custom_call" | custom-call | tf_op jit(solution)/shard_map/pallas_call | solution.py:426
  65.7 2.6 %shard_map.50 = (f32[256,256]{1,0:T(8,128)}, f32[256,128]{1,0:T(8,128)}, f32[4096,128]{1,0:T(8,128)}) custom-call(f32[256,256]{1,0:T(8,128)} %get-tuple-element.6.a, f32[256,128]{1,0:T(8,128)} %get-tuple-element.7.b, f32[4096,128]{1,0:T(8,128)} %get-tuple-element.8.c), custom_call_target="tpu_custom_call" | custom-call | tf_op jit(solution)/shard_map/pallas_call | solution.py:453
